TPU v7x, 768 devices: a whole 4x8x12 slice. The times are simulated.
768 devices in a mesh: dp: 48 (over z, y_lo), tensor: 16 (over x, y_hi, core).
Axes of the slice: x: 4, y: 8 (y_hi: 2, y_lo: 4; y = y_hi * 4 + y_lo), z: 12, core: 2. Of those that a mesh axis runs over, the one named last changes fastest.
Arguments:
- resid: bfloat16 [6144, 8192], P('dp', 'tensor'), may hold values from -6 to 6
- attn_out: bfloat16 [6144, 8192], P('dp', 'tensor'), may hold values from -6 to 6
- w_out: bfloat16 [8192, 8192], P('tensor'), may hold values from -0.0625 to 0.0625
- proj: bfloat16 [3072, 8192], P(None, 'tensor'), may hold values from -0.109375 to 0.109375
- student_in: bfloat16 [11520, 3072], P(('dp', 'tensor')), may hold values from -24 to 24
- dest: int32 [6144, 1], replicated, may hold values from 0 to 47; in each aligned block of 128 rows (0 to 127, 128 to 255, ...) at most 5 rows name the same one
Outputs:
- grad_proj: float32 [3072, 8192], P('dp', 'tensor')
Inputs may be any that keep to these rules, and one draw needn't show every extreme that they name: `dest`: within each aligned block of 128 rows (one teacher group) no student group is named by more than 5 rows, a bound that some block reaches.
All inputs are finite; a program needn't handle non-finite values.
Results may differ from a plain program's by a relative error of at most 0.0095.
Values may be sent and summed in bfloat16 or wider, within the bound.
No kernel may reach another device: no remote copies, remote signals or barrier semaphores. Data moves between devices by JAX's collectives and lax.ppermute only.
A program may use at most 64 MiB of HBM per device.

v0:
```python
import jax
import jax.numpy as jnp
from jax import lax
from jax.sharding import PartitionSpec as P


def local(resid, attn_out, w_out, proj, student_in, dest):
    row_total = attn_out.shape[0]
    col_width = attn_out.shape[1]
    groups = lax.axis_size("dp")
    my_group = lax.axis_index("dp")
    tensor_size = lax.axis_size("tensor")
    capacity = student_in.shape[0] * tensor_size // groups
    partial_sum = jnp.dot(attn_out, w_out, preferred_element_type=jnp.float32)
    summed = lax.psum_scatter(
        partial_sum.astype(jnp.bfloat16), "tensor", scatter_dimension=1, tiled=True
    ).astype(jnp.float32)
    hidden = (resid.astype(jnp.float32) + summed).astype(jnp.bfloat16)
    dest_table = dest[:, 0].reshape(groups, row_total)
    own_dest = lax.dynamic_slice_in_dim(dest[:, 0], my_group * row_total, row_total)
    group_iota = jnp.arange(groups, dtype=jnp.int32)
    onehot = (own_dest[:, None] == group_iota[None, :]).astype(jnp.int32)
    slot_rank = jnp.sum((jnp.cumsum(onehot, axis=0) - 1) * onehot, axis=1)
    slot_index = own_dest * capacity + slot_rank
    selector = (
        slot_index[None, :] == jnp.arange(groups * capacity, dtype=jnp.int32)[:, None]
    ).astype(jnp.bfloat16)
    packed = jnp.dot(selector, hidden, preferred_element_type=jnp.float32).astype(jnp.bfloat16)
    packed = packed.reshape(groups, capacity, col_width)
    arrived = lax.all_to_all(packed, "dp", split_axis=0, concat_axis=0, tiled=True).reshape(
        groups * capacity, col_width
    )
    counts = jnp.sum((dest_table == my_group).astype(jnp.int32), axis=1)
    valid_slot = (jnp.arange(capacity, dtype=jnp.int32)[None, :] < counts[:, None]).reshape(
        groups * capacity
    )
    whole_rows = lax.all_gather(student_in, "tensor", axis=0, tiled=True)
    predicted = jnp.dot(whole_rows, proj, preferred_element_type=jnp.float32)
    mismatch = (
        jnp.where(valid_slot[:, None], predicted - arrived.astype(jnp.float32), 0.0) / row_total
    ).astype(jnp.bfloat16)
    contract_rows = (((0,), (0,)), ((), ()))
    local_grad = lax.dot_general(
        whole_rows, mismatch, contract_rows, preferred_element_type=jnp.float32
    )
    grad_proj = lax.psum_scatter(local_grad, "dp", scatter_dimension=0, tiled=True)
    return grad_proj


def solution(mesh):
    return jax.shard_map(
        local,
        mesh=mesh,
        in_specs=(
            P("dp", "tensor"),
            P("dp", "tensor"),
            P("tensor", None),
            P(None, "tensor"),
            P(("dp", "tensor"), None),
            P(),
        ),
        out_specs=P("dp", "tensor"),
        check_vma=False,
    )
```

profile of v0, /device:TPU:6, one launch (start us, length us, event | category | flops | bytes accessed | tf_op | source)
XLA Modules:
  0.0 467.7 jit_solution(3836820546528011098)
XLA Ops:
  6.5 0.0 copy-start
  6.5 0.0 copy-start.1
  6.5 0.0 reduce-scatter.5.cloned.1.call-start
  6.5 6.2 %convolution_convert_fusion = bf16[128,8192]{1,0:T(8,128)(2,1)} fusion(bf16[128,512]{1,0:T(8,128)(2,1)} %param.7, bf16[512,8192]{1,0:T(8,128)(2,1)} %param.8), kind=kOutput, calls=%fused_computation | convolution fusion | flops 1074790400 | bytes 10616832 | tf_op jit(solution)/shard_map/dot_general | solution.py:14
  12.8 0.0 reduce-scatter.5.cloned.1.call-update
  12.8 0.0 all-gather.3.cloned.1.call-start
  12.8 0.7 all-gather.3.cloned.1.call-update
  13.6 0.7 dynamic-slice_bitcast_fusion
  14.2 0.1 fusion.6
  14.3 0.2 reduce_window_sum.11
  14.5 0.2 select_reduce_fusion
  14.7 0.7 multiply_add_fusion
  15.3 106.7 %reduce-scatter.5.cloned.1.call-done = bf16[128,512]{1,0:T(8,128)(2,1)} async-done(((bf16[128,8192]{1,0:T(8,128)(2,1)}), bf16[128,512]{1,0:T(8,128)(2,1)}) %reduce-scatter.5.cloned.1.call-update) | async-done | bytes 131088 | tf_op jit(solution)/shard_map/reduce_scatter | solution.py:15
  122.0 0.0 copy-done.1
  122.0 1.1 convolution_convert_fusion.1
  123.2 0.8 reshape.35
  124.0 12.2 %all-to-all-start = ((bf16[48,5,512]{2,1,0:T(8,128)(2,1)}), bf16[48,5,512]{2,1,0:T(8,128)(2,1)S(1)}, u32[]{:S(2)}, u32[]{:S(2)}) async-start(bf16[48,5,512]{2,1,0:T(8,128)(2,1)} %reshape.35), calls=%async_computation.1 | async-start | bytes 786432 | tf_op jit(solution)/shard_map/all_to_all | solution.py:30
  136.2 0.0 reduce-scatter.7.cloned.1.call-start
  136.3 1.4 compare_convert_fusion
  137.7 0.8 reduce_sum.18
  138.5 0.1 iota_compare_fusion.3
  138.6 0.1 lt.26
  138.7 54.2 %all-gather.3.cloned.1.call-done = bf16[16,15,3072]{2,1,0:T(8,128)(2,1)} async-done(((bf16[1,15,3072]{2,1,0:T(8,128)(2,1)}), bf16[16,15,3072]{2,1,0:T(8,128)(2,1)}) %all-gather.3.cloned.1.call-update) | async-done | bytes 1474576 | tf_op jit(solution)/shard_map/all_gather | solution.py:37
  193.0 2.5 reshape.39
  195.5 0.0 all-to-all-done
  195.5 0.9 reshape.37
  196.3 0.0 copy-done
  196.3 6.6 %convolution_bitcast_fusion = f32[3072,512]{0,1:T(8,128)} fusion(bf16[240,3072]{1,0:T(8,128)(2,1)} %reshape.39, f32[240,512]{1,0:T(8,128)} %reshape.37, bf16[3072,512]{1,0:T(8,128)(2,1)S(1)} %copy-done, pred[240]{0:T(512)(128)(4,1)S(1)} %lt.26), kind=kOutput, calls=%fused_computation.1 | convolution fusion | flops 1510440960 | bytes 11403504 | tf_op jit(solution)/shard_map/dot_general | solution.py:43
  202.9 6.5 %copy.10 = f32[3072,512]{1,0:T(8,128)} copy(f32[3072,512]{0,1:T(8,128)} %convolution_bitcast_fusion) | data formatting | bytes 12582912
  209.5 0.0 reduce-scatter.7.cloned.1.call-update
  209.5 251.7 %reduce-scatter.7.cloned.1.call-done = f32[64,512]{1,0:T(8,128)} async-done(((f32[3072,512]{1,0:T(8,128)}), f32[64,512]{1,0:T(8,128)}) %reduce-scatter.7.cloned.1.call-update) | async-done | bytes 131088 | tf_op jit(solution)/shard_map/reduce_scatter | solution.py:46
Async XLA Ops:
  6.5 189.8 %copy-start = (bf16[3072,512]{1,0:T(8,128)(2,1)S(1)}, bf16[3072,512]{1,0:T(8,128)(2,1)}, u32[]{:S(2)}) copy-start(bf16[3072,512]{1,0:T(8,128)(2,1)} %param.9) | copy-start | bytes 9437188
  6.5 115.5 %copy-start.1 = (bf16[128,512]{1,0:T(8,128)(2,1)S(1)}, bf16[128,512]{1,0:T(8,128)(2,1)}, u32[]{:S(2)}) copy-start(bf16[128,512]{1,0:T(8,128)(2,1)} %param.6) | copy-start | bytes 393220
  6.5 115.5 %reduce-scatter.5.cloned.1.call-start = ((), (), s32[]{:S(2)}) async-start(), calls=%async_computation.3 | async-start | bytes 2228224 | tf_op jit(solution)/shard_map/reduce_scatter | solution.py:15
  12.8 180.2 %all-gather.3.cloned.1.call-start = ((), (), s32[]{:S(2)}) async-start(), calls=%async_computation.4 | async-start | bytes 1671168 | tf_op jit(solution)/shard_map/all_gather | solution.py:37
  124.0 71.5 %all-to-all-start = ((bf16[48,5,512]{2,1,0:T(8,128)(2,1)}), bf16[48,5,512]{2,1,0:T(8,128)(2,1)S(1)}, u32[]{:S(2)}, u32[]{:S(2)}) async-start(bf16[48,5,512]{2,1,0:T(8,128)(2,1)} %reshape.35), calls=%async_computation.1 | async-start | bytes 786432 | tf_op jit(solution)/shard_map/all_to_all | solution.py:30
  136.2 324.9 %reduce-scatter.7.cloned.1.call-start = ((), (), s32[]{:S(2)}) async-start(), calls=%async_computation.5 | async-start | bytes 6422528 | tf_op jit(solution)/shard_map/reduce_scatter | solution.py:46
Sparse Core Ops, SparseCore 0:
  12.9 109.0 reduce-scatter.4
  125.9 67.0 all-gather.2
  209.6 251.5 reduce-scatter.6
where the time goes:
time: 468 us
  waiting for transfers between devices  413 us (88%)
  matrix products  14 us (3%)
  between operations  13.2 us (3%)
  starting transfers between devices  12.3 us (3%)
  local copies, waits for them, and re-layouts  11.5 us (2%)
    reduce_scatter x1, waiting for transfers between devices, local(): lax.psum_scatter(local_grad, 'dp', scatter_dimension=0, tiled=True)  252 us
    reduce_scatter x1, waiting for transfers between devices, local(): lax.psum_scatter(partial_sum.astype(jnp.bfloat16), 'tensor', scatter_dime...  107 us
    all_gather x1, waiting for transfers between devices, local(): whole_rows = lax.all_gather(student_in, 'tensor', axis=0, tiled=True)  54.2 us
    all_to_all x1, starting transfers between devices, local(): lax.all_to_all(packed, 'dp', split_axis=0, concat_axis=0, tiled=True)  12.2 us
  transfers between devices with their start and end apart: 4, of which 3 were waited for; matrix products, arithmetic and copies ran while one was open for 2% of the time, Pallas kernels for 0%

commit v1 on v0

v1 whole, which is shorter than its diff:
```python
import jax
import jax.numpy as jnp
from jax import lax
from jax.sharding import Mesh, PartitionSpec as P

bf16 = jnp.bfloat16
f32 = jnp.float32
AXES = ("z", "yl", "x", "yh", "core")
DP = ("z", "yl")
TENSOR = ("x", "yh", "core")
PAD = 8


def swap(value, axis):
    return lax.ppermute(value, axis, [(0, 1), (1, 0)])


def pick(value, index, axis=0):
    return lax.dynamic_index_in_dim(value, index, axis, keepdims=False)


def gather_pair(value, axis):
    other = swap(value, axis)
    me = lax.axis_index(axis)
    first = jnp.where(me == 0, value, other)
    second = jnp.where(me == 0, other, value)
    return jnp.stack([first, second])


def gather_tensor(value):
    value = gather_pair(value, "yh")
    value = lax.all_gather(value, "x", axis=0, tiled=False)
    value = gather_pair(value, "core")
    return jnp.moveaxis(value, 0, 2)


def local(resid, attn_out, w_out, proj, student_in, dest):
    n_z, n_yl = lax.axis_size("z"), lax.axis_size("yl")
    n_x, n_yh, n_c = lax.axis_size("x"), lax.axis_size("yh"), lax.axis_size("core")
    groups = n_z * n_yl
    n_t = n_x * n_yh * n_c
    my_group = lax.axis_index(DP)
    my_yl, my_yh, my_core = lax.axis_index("yl"), lax.axis_index("yh"), lax.axis_index("core")
    rows, width = attn_out.shape
    own, ds = student_in.shape
    cap = own * n_t // groups
    per = groups // n_t

    padded = jnp.pad(student_in, ((0, 1), (0, 0)))
    slots = own + 1
    whole = gather_tensor(padded).reshape(n_t * slots, ds)
    quarters = padded.reshape(slots, n_z, n_yl, ds // groups).transpose(2, 0, 1, 3)
    quarters = quarters.reshape(n_yl, slots, ds // n_yl)
    quarter = lax.all_to_all(quarters, "yl", 0, 0, tiled=True)
    quarter = gather_tensor(quarter).reshape(n_t * n_yl * slots, ds // n_yl)

    partial = jnp.dot(attn_out, w_out, preferred_element_type=f32).astype(bf16)
    partial = partial.reshape(rows, n_x, n_yh, n_c, width)
    given = pick(partial, 1 - my_core, 3)
    kept = pick(partial, my_core, 3)
    summed = kept.astype(f32) + swap(given, "core").astype(f32)
    summed = summed.astype(bf16).transpose(1, 2, 0, 3)
    summed = lax.all_to_all(summed, "x", 0, 0, tiled=True)
    summed = jnp.sum(summed.astype(f32), axis=0)
    given = pick(summed, 1 - my_yh).astype(bf16)
    kept = pick(summed, my_yh)
    hidden = (resid.astype(f32) + kept + swap(given, "yh").astype(f32)).astype(bf16)

    dest_table = dest[:, 0].reshape(groups, rows)
    own_dest = pick(dest_table, my_group)
    row_iota = jnp.arange(rows, dtype=jnp.int32)
    same = (own_dest[:, None] == own_dest[None, :]) & (row_iota[None, :] < row_iota[:, None])
    slot_rank = jnp.sum(same.astype(jnp.int32), axis=1)
    slot_index = own_dest * PAD + slot_rank
    selector = (
        slot_index[None, :] == jnp.arange(groups * PAD, dtype=jnp.int32)[:, None]
    ).astype(bf16)
    packed = jnp.dot(selector, hidden, preferred_element_type=f32).astype(bf16)
    arrived = lax.all_to_all(
        packed.reshape(groups, PAD, width), DP, 0, 0, tiled=True
    ).reshape(groups * PAD, width)
    slot = jnp.arange(n_t * slots, dtype=jnp.int32)
    part, place = slot // slots, slot % slots
    origin = jnp.where(place < own, (part * per + place // cap) * PAD + place % cap, -1)
    placing = (origin[:, None] == jnp.arange(groups * PAD, dtype=jnp.int32)[None, :]).astype(bf16)
    targets = jnp.dot(placing, arrived, preferred_element_type=f32)
    counts = jnp.sum((dest_table == my_group).astype(jnp.int32), axis=1)
    filled = (jnp.arange(PAD, dtype=jnp.int32)[None, :] < counts[:, None]).reshape(groups * PAD)
    valid = jnp.dot(placing, filled.astype(bf16)[:, None], preferred_element_type=f32) > 0.5

    predicted = jnp.dot(whole, proj, preferred_element_type=f32)
    mismatch = (jnp.where(valid, predicted - targets, 0.0) / rows).astype(bf16)

    mismatch = lax.all_gather(mismatch.reshape(n_t, slots, width), "yl", axis=1)
    mismatch = mismatch.reshape(n_t * n_yl * slots, width)
    partial_grad = lax.dot_general(
        quarter, mismatch, (((0,), (0,)), ((), ())), preferred_element_type=f32
    ).astype(bf16)
    partial_grad = lax.all_to_all(
        partial_grad.reshape(n_z, ds // groups, width), "z", 0, 0, tiled=True
    )
    return jnp.sum(partial_grad.astype(f32), axis=0)


def solution(mesh):
    fine = Mesh(mesh.devices.reshape(12, 4, 4, 2, 2), AXES)
    return jax.shard_map(
        local,
        mesh=fine,
        in_specs=(
            P(DP, TENSOR),
            P(DP, TENSOR),
            P(TENSOR, None),
            P(None, TENSOR),
            P(DP + TENSOR, None),
            P(),
        ),
        out_specs=P(DP, TENSOR),
        check_vma=False,
    )
```

time: 468 us -> 225 us (0.48)
  waiting for transfers between devices: 413 us -> 28.5 us
  blocking collectives: 0 us -> 78.4 us
  starting transfers between devices: 12.3 us -> 55.2 us
  other arithmetic: 3.38 us -> 14.2 us
  local copies, waits for them, and re-layouts: 11.5 us -> 19.7 us
    reduce_scatter x2 -> x0, waiting for transfers between devices: 358 us -> none  [the longest x1 252 us: local(): lax.psum_scatter(local_grad, 'dp', scatter_dimension=0, tiled=True)]
    all_gather x1, waiting for transfers between devices: 54.2 us -> 10.8 us  [local(): mismatch = lax.all_gather(mismatch.reshape(n_t, slots, width), 'yl', axis=1)]
    all_to_all x0 -> x1, blocking collectives: none -> 42.2 us  [local(): lax.all_to_all(partial_grad.reshape(n_z, ds // groups, width), 'z', 0, 0,...]
    all_gather x0 -> x2, blocking collectives: none -> 36.2 us  [gather_tensor(): value = lax.all_gather(value, 'x', axis=0, tiled=False)]
    ppermute x0 -> x6, starting transfers between devices: none -> 24.4 us  [swap(): return lax.ppermute(value, axis, [(0, 1), (1, 0)])]
    all_to_all x1 -> x3, starting transfers between devices: 12.2 us -> 30.6 us  [the longest x1 18.8 us: local(): lax.all_to_all(packed.reshape(groups, PAD, width), DP, 0, 0, tiled=True)]
    all_to_all x1 -> x3, waiting for transfers between devices: 0.01 us -> 14.9 us  [the longest x1 14.9 us: local(): lax.all_to_all(packed.reshape(groups, PAD, width), DP, 0, 0, tiled=True)]
    dynamic_slice x1, local copies, waits for them, and re-layouts: 0.66 us -> 7.99 us  [pick(): return lax.dynamic_index_in_dim(value, index, axis, keepdims=False)]
  transfers between devices with their start and end apart: 4 -> 10, of which waited for: 3 -> 4; matrix products, arithmetic and copies ran while one was open for 2% -> 9% of each run, Pallas kernels for 0% -> 0%
where the time goes in v1:
time: 225 us; the launch traced here: 224 us
  blocking collectives  78.4 us (35%)
  starting transfers between devices  55.2 us (25%)
  waiting for transfers between devices  28.5 us (13%)
  local copies, waits for them, and re-layouts  19.7 us (9%)
  matrix products  14.6 us (6%)
  other arithmetic  14.2 us (6%)
  between operations  13.6 us (6%)
    all_to_all x1, blocking collectives, local(): lax.all_to_all(partial_grad.reshape(n_z, ds // groups, width), 'z', 0, 0,...  42.2 us
    all_gather x2, blocking collectives, gather_tensor(): value = lax.all_gather(value, 'x', axis=0, tiled=False)  36.2 us
    ppermute x6, starting transfers between devices, swap(): return lax.ppermute(value, axis, [(0, 1), (1, 0)])  24.4 us
    all_to_all x1, starting transfers between devices, local(): lax.all_to_all(packed.reshape(groups, PAD, width), DP, 0, 0, tiled=True)  18.8 us
    all_to_all x1, waiting for transfers between devices, local(): lax.all_to_all(packed.reshape(groups, PAD, width), DP, 0, 0, tiled=True)  14.9 us
    all_gather x1, waiting for transfers between devices, local(): mismatch = lax.all_gather(mismatch.reshape(n_t, slots, width), 'yl', axis=1)  10.8 us
    dynamic_slice x1, local copies, waits for them, and re-layouts, pick(): return lax.dynamic_index_in_dim(value, index, axis, keepdims=False)  7.99 us
    all_to_all x1, starting transfers between devices, local(): summed = lax.all_to_all(summed, 'x', 0, 0, tiled=True)  7.88 us
  transfers between devices with their start and end apart: 10, of which 4 were waited for; matrix products, arithmetic and copies ran while one was open for 9% of the time, Pallas kernels for 0%

profile of v1, /device:TPU:6, one launch (start us, length us, event | category | flops | bytes accessed | tf_op | source)
XLA Modules:
  0.0 224.2 jit_solution(1615839471235218199)
XLA Ops:
  6.5 6.2 %convolution_convert_fusion = bf16[128,8192]{1,0:T(8,128)(2,1)} fusion(bf16[128,512]{1,0:T(8,128)(2,1)} %param.7, bf16[512,8192]{1,0:T(8,128)(2,1)} %param.8), kind=kOutput, calls=%fused_computation | convolution fusion | flops 1074790400 | bytes 10616832 | tf_op jit(solution)/shard_map/dot_general | solution.py:57
  12.7 4.5 %reshape.87 = bf16[128,4,2,2,512]{4,3,2,1,0:T(2,128)(2,1)} reshape(bf16[128,8192]{1,0:T(8,128)(2,1)} %convolution_convert_fusion) | data formatting | bytes 4194304 | tf_op jit(solution)/shard_map/reshape | solution.py:58
  17.2 8.0 %constant_dynamic-slice_fusion.1 = (bf16[128,4,2,1,512]{4,3,2,1,0:T(2,128)(2,1)}, bf16[128,4,2,1,512]{4,3,2,1,0:T(2,128)(2,1)S(1)}) fusion(bf16[128,4,2,2,512]{4,3,2,1,0:T(2,128)(2,1)} %reshape.87, s32[]{:T(128)S(6)} %select_n.141, s32[]{:T(128)S(6)} %select_n.142), kind=kLoop, calls=%fused_computation.58 | loop fusion | bytes 4194312 | tf_op jit(solution)/shard_map/jit(dynamic_index_in_dim)/dynamic_slice | solution.py:19
  25.2 2.1 copy.32
  27.3 1.9 collective-permute-start.4
  29.3 0.7 pad.4
  29.9 7.7 %collective-permute-start.2 = (bf16[16,3072]{1,0:T(8,128)(2,1)}, bf16[16,3072]{1,0:T(8,128)(2,1)}, u32[]{:S(2)}, u32[]{:S(2)}) collective-permute-start(bf16[16,3072]{1,0:T(8,128)(2,1)} %pad.4), channel_id=1, source_target_pairs={{0,2},{2,0},{1,3},{3,1},{4,6},{6,4},{5,7},{7,5},{8,10},{10,8},{9,1... | collective-permute-start | bytes 294920 | tf_op jit(solution)/shard_map/ppermute | solution.py:15
  37.7 0.1 convert_reduce_fusion.3
  37.8 1.8 reshape.83
  39.6 0.1 iota_compare_fusion.6
  39.6 0.1 reshape.95
  39.7 1.0 copy.33
  40.7 0.8 reshape.84
  41.5 0.2 convert_reduce_fusion.2
  41.7 0.2 fusion.8
  42.0 0.0 collective-permute-done.4
  42.0 4.1 %fusion.5 = bf16[4,2,128,512]{3,2,1,0:T(8,128)(2,1)} fusion(bf16[128,4,2,512]{3,0,2,1:T(8,128)(2,1)} %collective-permute-done.4, bf16[128,4,2,1,512]{4,3,2,1,0:T(2,128)(2,1)} %get-tuple-element.5), kind=kLoop, calls=%fused_computation.14 | loop fusion | flops 2097152 | bytes 3145728 | tf_op jit(solution)/shard_map/transpose | solution.py:62
  46.1 7.9 %all-to-all-start.1 = ((bf16[4,2,128,512]{3,2,1,0:T(8,128)(2,1)}), bf16[4,2,128,512]{3,2,1,0:T(8,128)(2,1)}, u32[]{:S(2)}, u32[]{:S(2)}) async-start(bf16[4,2,128,512]{3,2,1,0:T(8,128)(2,1)} %fusion.5), calls=%async_computation.1 | async-start | bytes 2097152 | tf_op jit(solution)/shard_map/all_to_all | solution.py:63
  54.0 1.0 select_bitcast_fusion.5
  55.0 22.4 %all-gather.1 = bf16[8,16,3072]{2,1,0:T(8,128)(2,1)} all-gather(bf16[2,16,3072]{2,1,0:T(8,128)(2,1)S(1)} %pad_maximum_fusion.3), channel_id=3, replica_groups=mesh['z'=12,'yl'=4,'x'=4,'yh'=2,'core'=2] {'x'}, dimensions={0}, use_global_device_ids=true | all-gather | bytes 983040 | tf_op jit(solution)/shard_map/all_gather | solution.py:32
  77.3 1.9 collective-permute-start.3
  79.2 3.9 %all-to-all-start = ((bf16[4,16,768]{2,1,0:T(8,128)(2,1)}), bf16[4,16,768]{2,1,0:T(8,128)(2,1)}, u32[]{:S(2)}, u32[]{:S(2)}) async-start(bf16[4,16,768]{2,1,0:T(8,128)(2,1)} %reshape.84), calls=%async_computation | async-start | bytes 196608 | tf_op jit(solution)/shard_map/all_to_all | solution.py:54
  83.2 1.4 convert_reduce_fusion
  84.6 0.8 copy-done.1
  85.4 7.8 %collective-permute-start.5 = (bf16[128,512]{1,0:T(8,128)(2,1)S(1)}, bf16[128,512]{1,0:T(8,128)(2,1)S(1)}, u32[]{:S(2)}, u32[]{:S(2)}) collective-permute-start(bf16[128,512]{1,0:T(8,128)(2,1)S(1)} %fusion.13), channel_id=1, source_target_pairs={{0,2},{2,0},{1,3},{3,1},{4,6},{6,4},{5,7},{7,5},{8,10},{10,8},{9,1... | collective-permute-start | bytes 393224 | tf_op jit(solution)/shard_map/ppermute | solution.py:15
  93.2 0.7 fusion.24
  94.0 3.1 %collective-permute-start = (bf16[4,16,768]{2,1,0:T(8,128)(2,1)}, bf16[4,16,768]{2,1,0:T(8,128)(2,1)}, u32[]{:S(2)}, u32[]{:S(2)}) collective-permute-start(bf16[4,16,768]{2,1,0:T(8,128)(2,1)} %all-to-all-done), channel_id=1, source_target_pairs={{0,2},{2,0},{1,3},{3,1},{4,6},{6,4},{5,7},{7,5},{8,10},{10,8},{9,1... | collective-permute-start | bytes 294920 | tf_op jit(solution)/shard_map/ppermute | solution.py:15
  97.1 0.4 collective-permute-done.5
  97.5 2.0 fusion.4
  99.5 18.8 %all-to-all-start.2 = ((bf16[48,8,512]{2,1,0:T(8,128)(2,1)}), bf16[48,8,512]{2,1,0:T(8,128)(2,1)S(1)}, u32[]{:S(2)}, u32[]{:S(2)}) async-start(bf16[48,8,512]{2,1,0:T(8,128)(2,1)} %fusion.4), calls=%async_computation.2 | async-start | bytes 786432 | tf_op jit(solution)/shard_map/all_to_all | solution.py:79
  118.3 0.2 all-gather.4.cloned.1.call-start
  118.5 1.6 select_bitcast_fusion.7
  120.1 1.5 select_bitcast_fusion.1
  121.6 1.3 pad_maximum_fusion.1
  122.9 14.9 %all-to-all-done.2 = bf16[48,8,512]{2,1,0:T(8,128)(2,1)S(1)} async-done(((bf16[48,8,512]{2,1,0:T(8,128)(2,1)}), bf16[48,8,512]{2,1,0:T(8,128)(2,1)S(1)}, u32[]{:S(2)}, u32[]{:S(2)}) %all-to-all-start.2) | async-done | bytes 393248 | tf_op jit(solution)/shard_map/all_to_all | solution.py:79
  137.9 0.3 fusion.6
  138.2 0.0 copy-start.3
  138.2 3.1 %fusion.3 = bf16[256,512]{1,0:T(8,128)(2,1)} fusion(f32[256,512]{1,0:T(8,128)S(1)} %fusion.6, bf16[256,3072]{1,0:T(8,128)(2,1)} %bitcast.79, bf16[3072,512]{1,0:T(8,128)(2,1)S(1)} %copy-done, pred[256]{0:T(512)(128)(4,1)S(1)} %broadcast_compare_fusion), kind=kOutput, calls=%fused_computation.12 | convolution fusion | flops 805830656 | bytes 5505280 | tf_op jit(solution)/shard_map/dot_general | solution.py:91
  141.4 0.0 all-gather.4.cloned.1.call-update
  141.5 13.9 %all-gather = bf16[8,4,16,768]{3,2,1,0:T(8,128)(2,1)S(1)} all-gather(bf16[2,4,16,768]{3,2,1,0:T(8,128)(2,1)S(1)} %pad_maximum_fusion.2), channel_id=2, replica_groups=mesh['z'=12,'yl'=4,'x'=4,'yh'=2,'core'=2] {'x'}, dimensions={0}, use_global_device_ids=true | all-gather | bytes 983040 | tf_op jit(solution)/shard_map/all_gather | solution.py:32
  155.3 1.9 collective-permute-start.1
  157.2 2.3 %collective-permute-done.1 = bf16[4,2,4,16,768]{4,3,2,1,0:T(8,128)(2,1)S(1)} collective-permute-done((bf16[4,2,4,16,768]{4,3,2,1,0:T(8,128)(2,1)S(1)}, bf16[4,2,4,16,768]{4,3,2,1,0:T(8,128)(2,1)S(1)}, u32[]{:S(2)}, u32[]{:S(2)}) %collective-permute-start.1) | collective-permute-done | bytes 786464 | tf_op jit(solution)/shard_map/ppermute | solution.py:15
  159.5 0.1 select_bitcast_fusion.3
  159.6 1.3 pad_maximum_fusion
  160.9 10.8 %all-gather.4.cloned.1.call-done = bf16[16,4,16,512]{3,2,1,0:T(8,128)(2,1)} async-done(((bf16[16,1,16,512]{3,2,1,0:T(8,128)(2,1)}), bf16[16,4,16,512]{3,2,1,0:T(8,128)(2,1)}) %all-gather.4.cloned.1.call-update) | async-done | bytes 1048592 | tf_op jit(solution)/shard_map/all_gather | solution.py:94
  171.7 2.7 %convolution_convert_fusion.1 = bf16[768,512]{1,0:T(8,128)(2,1)S(1)} fusion(bf16[1024,768]{1,0:T(8,128)(2,1)} %bitcast.80, bf16[1024,512]{1,0:T(8,128)(2,1)} %bitcast.87), kind=kOutput, calls=%fused_computation.7 | convolution fusion | flops 805699584 | bytes 3407872 | tf_op jit(solution)/shard_map/dot_general | solution.py:96
  174.4 42.2 %all_to_all.20 = bf16[12,64,512]{2,1,0:T(8,128)(2,1)S(1)} all-to-all(bf16[12,64,512]{2,1,0:T(8,128)(2,1)S(1)} %bitcast.82), channel_id=1, replica_groups=mesh['z'=12,'yl'=4,'x'=4,'yh'=2,'core'=2] {'z'}, dimensions={0} | all-to-all | bytes 1572864 | tf_op jit(solution)/shard_map/all_to_all | solution.py:99
  216.6 0.8 convert_reduce_fusion.1
  (23 shorter events, 0.1 us)
Async XLA Ops:
  6.5 131.7 %copy-start = (bf16[3072,512]{1,0:T(8,128)(2,1)S(1)}, bf16[3072,512]{1,0:T(8,128)(2,1)}, u32[]{:S(2)}) copy-start(bf16[3072,512]{1,0:T(8,128)(2,1)} %param.9) | copy-start | bytes 9437188
  25.2 4.0 %copy-start.2 = (bf16[15,3072]{1,0:T(8,128)(2,1)S(1)}, bf16[15,3072]{1,0:T(8,128)(2,1)}, u32[]{:S(2)}) copy-start(bf16[15,3072]{1,0:T(8,128)(2,1)} %param.10) | copy-start | bytes 276484
  25.2 12.4 %copy-start.6 = (s32[6144,1]{0,1:T(1,128)S(1)}, s32[6144,1]{0,1:T(1,128)}, u32[]{:S(2)}) copy-start(s32[6144,1]{0,1:T(1,128)} %param.11) | copy-start | bytes 73732
  27.3 14.7 %collective-permute-start.4 = (bf16[128,4,2,512]{3,0,2,1:T(8,128)(2,1)}, bf16[128,4,2,512]{3,0,2,1:T(8,128)(2,1)}, u32[]{:S(2)}, u32[]{:S(2)}) collective-permute-start(bf16[128,4,2,512]{3,0,2,1:T(8,128)(2,1)} %bitcast.75), channel_id=1, source_target_pairs={{0,1},{1,0},{2,3},{3,2},{4,5},{5,4},{6,7},{7,6},{8,9},{9,8},{10,11... | collective-permute-start | bytes 3145736 | tf_op jit(solution)/shard_map/ppermute | solution.py:15
  29.9 24.1 %collective-permute-start.2 = (bf16[16,3072]{1,0:T(8,128)(2,1)}, bf16[16,3072]{1,0:T(8,128)(2,1)}, u32[]{:S(2)}, u32[]{:S(2)}) collective-permute-start(bf16[16,3072]{1,0:T(8,128)(2,1)} %pad.4), channel_id=1, source_target_pairs={{0,2},{2,0},{1,3},{3,1},{4,6},{6,4},{5,7},{7,5},{8,10},{10,8},{9,1... | collective-permute-start | bytes 294920 | tf_op jit(solution)/shard_map/ppermute | solution.py:15
  46.1 33.2 %all-to-all-start.1 = ((bf16[4,2,128,512]{3,2,1,0:T(8,128)(2,1)}), bf16[4,2,128,512]{3,2,1,0:T(8,128)(2,1)}, u32[]{:S(2)}, u32[]{:S(2)}) async-start(bf16[4,2,128,512]{3,2,1,0:T(8,128)(2,1)} %fusion.5), calls=%async_computation.1 | async-start | bytes 2097152 | tf_op jit(solution)/shard_map/all_to_all | solution.py:63
  54.0 43.5 %copy-start.5 = (bf16[128,512]{1,0:T(8,128)(2,1)S(1)}, bf16[128,512]{1,0:T(8,128)(2,1)}, u32[]{:S(2)}) copy-start(bf16[128,512]{1,0:T(8,128)(2,1)} %param.6) | copy-start | bytes 393220
  77.3 42.8 %collective-permute-start.3 = (bf16[4,2,16,3072]{3,2,1,0:T(8,128)(2,1)}, bf16[4,2,16,3072]{3,2,1,0:T(8,128)(2,1)}, u32[]{:S(2)}, u32[]{:S(2)}) collective-permute-start(bf16[4,2,16,3072]{3,2,1,0:T(8,128)(2,1)} %bitcast.13), channel_id=1, source_target_pairs={{0,1},{1,0},{2,3},{3,2},{4,5},{5,4},{6,7},{7,6},{8,9},{9,8},{10,11... | collective-permute-start | bytes 2359304 | tf_op jit(solution)/shard_map/ppermute | solution.py:15
  79.2 14.7 %all-to-all-start = ((bf16[4,16,768]{2,1,0:T(8,128)(2,1)}), bf16[4,16,768]{2,1,0:T(8,128)(2,1)}, u32[]{:S(2)}, u32[]{:S(2)}) async-start(bf16[4,16,768]{2,1,0:T(8,128)(2,1)} %reshape.84), calls=%async_computation | async-start | bytes 196608 | tf_op jit(solution)/shard_map/all_to_all | solution.py:54
  84.6 0.8 copy-start.1
  85.4 12.1 %collective-permute-start.5 = (bf16[128,512]{1,0:T(8,128)(2,1)S(1)}, bf16[128,512]{1,0:T(8,128)(2,1)S(1)}, u32[]{:S(2)}, u32[]{:S(2)}) collective-permute-start(bf16[128,512]{1,0:T(8,128)(2,1)S(1)} %fusion.13), channel_id=1, source_target_pairs={{0,2},{2,0},{1,3},{3,1},{4,6},{6,4},{5,7},{7,5},{8,10},{10,8},{9,1... | collective-permute-start | bytes 393224 | tf_op jit(solution)/shard_map/ppermute | solution.py:15
  94.0 24.5 %collective-permute-start = (bf16[4,16,768]{2,1,0:T(8,128)(2,1)}, bf16[4,16,768]{2,1,0:T(8,128)(2,1)}, u32[]{:S(2)}, u32[]{:S(2)}) collective-permute-start(bf16[4,16,768]{2,1,0:T(8,128)(2,1)} %all-to-all-done), channel_id=1, source_target_pairs={{0,2},{2,0},{1,3},{3,1},{4,6},{6,4},{5,7},{7,5},{8,10},{10,8},{9,1... | collective-permute-start | bytes 294920 | tf_op jit(solution)/shard_map/ppermute | solution.py:15
  99.5 38.4 %all-to-all-start.2 = ((bf16[48,8,512]{2,1,0:T(8,128)(2,1)}), bf16[48,8,512]{2,1,0:T(8,128)(2,1)S(1)}, u32[]{:S(2)}, u32[]{:S(2)}) async-start(bf16[48,8,512]{2,1,0:T(8,128)(2,1)} %fusion.4), calls=%async_computation.2 | async-start | bytes 786432 | tf_op jit(solution)/shard_map/all_to_all | solution.py:79
  118.3 53.5 %all-gather.4.cloned.1.call-start = ((), (), s32[]{:S(2)}) async-start(), calls=%async_computation.4 | async-start | bytes 1310720 | tf_op jit(solution)/shard_map/all_gather | solution.py:94
  138.2 3.2 %copy-start.3 = (bf16[1,4,16,768]{3,2,1,0:T(8,128)(2,1)S(1)}, bf16[1,4,16,768]{3,2,1,0:T(8,128)(2,1)}, u32[]{:S(2)}) copy-start(bf16[1,4,16,768]{3,2,1,0:T(8,128)(2,1)} %get-tuple-element.13) | copy-start | bytes 294916
  138.2 3.2 %copy-start.4 = (bf16[1,4,16,768]{3,2,1,0:T(8,128)(2,1)S(1)}, bf16[1,4,16,768]{3,2,1,0:T(8,128)(2,1)}, u32[]{:S(2)}) copy-start(bf16[1,4,16,768]{3,2,1,0:T(8,128)(2,1)} %get-tuple-element.14) | copy-start | bytes 294916
  155.3 4.2 %collective-permute-start.1 = (bf16[4,2,4,16,768]{4,3,2,1,0:T(8,128)(2,1)S(1)}, bf16[4,2,4,16,768]{4,3,2,1,0:T(8,128)(2,1)S(1)}, u32[]{:S(2)}, u32[]{:S(2)}) collective-permute-start(bf16[4,2,4,16,768]{4,3,2,1,0:T(8,128)(2,1)S(1)} %bitcast.77), channel_id=1, source_target_pairs={{0,1},{1,0},{2,3},{3,2},{4,5},{5,4},{6,7},{7,6},{8,9},{9,8},{10,11... | collective-permute-start | bytes 2359304 | tf_op jit(solution)/shard_map/ppermute | solution.py:15
Sparse Core Ops, SparseCore 0:
  141.5 30.1 all-gather.3

commit v2 on v1

v2 whole, which is shorter than its diff:
```python
import jax
import jax.numpy as jnp
from jax import lax
from jax.experimental import pallas as pl
from jax.experimental.pallas import tpu as pltpu
from jax.sharding import Mesh, PartitionSpec as P

bf16 = jnp.bfloat16
f32 = jnp.float32
AXES = ("z", "yl", "x", "yh", "core")
DP = ("z", "yl")
TENSOR = ("x", "yh", "core")
PAD = 8


def meet(value, axis, bit):
    return lax.ppermute(value, axis, [(i, i ^ bit) for i in range(lax.axis_size(axis))])


def joined(value, axis, bit):
    return jnp.concatenate([value, meet(value, axis, bit)], axis=0)


def shift(value, axis, step):
    size = lax.axis_size(axis)
    return lax.ppermute(value, axis, [(i, (i + step) % size) for i in range(size)])


def pick(value, index, axis=0):
    return lax.dynamic_index_in_dim(value, index, axis, keepdims=False)


def after(value, other):
    return lax.optimization_barrier((value, other))[0]


def product_kernel(core_ref, rows_ref, weight_ref, *refs):
    *added, out_ref, held, arrived = refs
    blocks, _, width = held.shape
    copies = []
    for k in range(blocks):
        first = pl.multiple_of((2 * k + core_ref[0]) * width, width)
        copies.append(
            pltpu.make_async_copy(weight_ref.at[:, pl.ds(first, width)], held.at[k], arrived.at[k])
        )
    for copy in copies:
        copy.start()
    for k, copy in enumerate(copies):
        copy.wait()
        block = jnp.dot(rows_ref[...], held[k], preferred_element_type=f32)
        for ref in added:
            block = block + ref[k].astype(f32)
        out_ref[k] = block.astype(bf16)


def half_product(rows, weight, core, blocks, *added):
    n, depth = rows.shape
    width = weight.shape[1] // (2 * blocks)
    return pl.pallas_call(
        product_kernel,
        in_specs=[
            pl.BlockSpec(memory_space=pltpu.SMEM),
            pl.BlockSpec(memory_space=pltpu.VMEM),
            pl.BlockSpec(memory_space=pltpu.HBM),
        ]
        + [pl.BlockSpec(memory_space=pltpu.VMEM) for _ in added],
        out_specs=pl.BlockSpec(memory_space=pltpu.VMEM),
        out_shape=jax.ShapeDtypeStruct((blocks, n, width), bf16),
        scratch_shapes=[
            pltpu.VMEM((blocks, depth, width), bf16),
            pltpu.SemaphoreType.DMA((blocks,)),
        ],
        cost_estimate=pl.CostEstimate(
            flops=2 * n * depth * width * blocks,
            bytes_accessed=2 * blocks * width * (depth + n),
            transcendentals=0,
        ),
        compiler_params=pltpu.CompilerParams(vmem_limit_bytes=52 * 1024 * 1024),
    )(core.reshape(1), rows, weight, *added)


def local(resid, attn_out, w_out, proj, student_in, dest):
    n_z, n_yl = lax.axis_size("z"), lax.axis_size("yl")
    n_x, n_yh, n_c = lax.axis_size("x"), lax.axis_size("yh"), lax.axis_size("core")
    groups = n_z * n_yl
    n_t = n_x * n_yh * n_c
    my_group = lax.axis_index(DP)
    my_yl, my_x = lax.axis_index("yl"), lax.axis_index("x")
    my_yh, my_core = lax.axis_index("yh"), lax.axis_index("core")
    rows, width = attn_out.shape
    own, ds = student_in.shape
    cap = own * n_t // groups
    per = groups // n_t
    slots = own + 1
    part = ds // n_yl

    given = half_product(attn_out, w_out, 1 - my_core, n_x * n_yh)
    taken = meet(given, "core", 1)

    whole = jnp.pad(student_in, ((0, 1), (0, 0)))
    whole = whole.reshape(slots, n_z, n_yl, ds // groups).transpose(0, 2, 1, 3).reshape(slots, ds)
    whole = joined(whole, "yh", 1)

    slot = jnp.arange(n_t * slots, dtype=jnp.int32)
    place, order = slot % slots, slot // slots
    from_yh = my_yh ^ (order % n_yh)
    from_x = my_x ^ (order // n_yh % n_x)
    from_core = my_core ^ (order // (n_yh * n_x))
    holder = (from_x * n_yh + from_yh) * n_c + from_core
    origin = jnp.where(place < own, (holder * per + place // cap) * PAD + place % cap, -1)
    placing = (origin[:, None] == jnp.arange(groups * PAD, dtype=jnp.int32)[None, :]).astype(bf16)
    dest_table = dest[:, 0].reshape(groups, rows)
    counts = jnp.sum((dest_table == my_group).astype(jnp.int32), axis=1)
    filled = (jnp.arange(PAD, dtype=jnp.int32)[None, :] < counts[:, None]).reshape(groups * PAD)
    valid = jnp.dot(placing, filled.astype(bf16)[:, None], preferred_element_type=f32) > 0.5
    own_dest = pick(dest_table, my_group)
    row_iota = jnp.arange(rows, dtype=jnp.int32)
    same = (own_dest[:, None] == own_dest[None, :]) & (row_iota[None, :] < row_iota[:, None])
    slot_rank = jnp.sum(same.astype(jnp.int32), axis=1)
    slot_index = own_dest * PAD + slot_rank
    selector = (
        slot_index[None, :] == jnp.arange(groups * PAD, dtype=jnp.int32)[:, None]
    ).astype(bf16)

    summed = half_product(attn_out, w_out, my_core, n_x * n_yh, taken)
    summed, whole = lax.optimization_barrier((summed, whole))
    whole = joined(whole, "x", 1)

    def lanes(k):
        first = lax.rem(my_yl + k, n_yl) * part
        return lax.dynamic_slice_in_dim(whole, first, part, 1)

    quarter = [lanes(0)] + [shift(lanes(k), "yl", k) for k in range(1, n_yl)]
    weight = after(proj, whole).reshape(n_z, n_yl, ds // groups, width).transpose(1, 0, 2, 3)
    summed = summed.reshape(n_x, n_yh * rows, width)
    summed = lax.all_to_all(summed, "x", 0, 0, tiled=True)
    summed = jnp.sum(summed.astype(f32), axis=0).reshape(n_yh, rows, width)
    given = pick(summed, 1 - my_yh).astype(bf16)
    kept = resid.astype(f32) + pick(summed, my_yh)
    given, whole = lax.optimization_barrier((given, whole))
    taken = meet(given, "yh", 1)
    whole = joined(whole, "x", 2)
    taken, whole = lax.optimization_barrier((taken, whole))
    hidden = (kept + taken.astype(f32)).astype(bf16)

    packed = jnp.dot(selector, hidden, preferred_element_type=f32).astype(bf16)
    quarter = joined(after(jnp.concatenate(quarter, axis=1), packed), "x", 2)
    whole = joined(after(whole, packed), "core", 1)
    predicted = jnp.dot(whole, weight.reshape(ds, width), preferred_element_type=f32)
    arrived = lax.all_to_all(
        packed.reshape(groups, PAD, width), DP, 0, 0, tiled=True
    ).reshape(groups * PAD, width)
    targets = jnp.dot(placing, arrived, preferred_element_type=f32)
    mismatch = (jnp.where(valid, predicted - targets, 0.0) / rows).astype(bf16)

    quarter = joined(after(quarter, arrived), "core", 1)
    mismatches = [mismatch] + [shift(mismatch, "yl", k) for k in range(1, n_yl)]
    partial_grad = sum(
        lax.dot_general(
            quarter[:, k * part : (k + 1) * part],
            mismatches[k],
            (((0,), (0,)), ((), ())),
            preferred_element_type=f32,
        )
        for k in range(n_yl)
    )
    partial_grad = lax.all_to_all(
        partial_grad.astype(bf16).reshape(n_z, ds // groups, width), "z", 0, 0, tiled=True
    )
    return jnp.sum(partial_grad.astype(f32), axis=0)


def solution(mesh):
    fine = Mesh(mesh.devices.reshape(12, 4, 4, 2, 2), AXES)
    return jax.shard_map(
        local,
        mesh=fine,
        in_specs=(
            P(DP, TENSOR),
            P(DP, TENSOR),
            P(TENSOR, None),
            P(None, TENSOR),
            P(DP + TENSOR, None),
            P(),
        ),
        out_specs=P(DP, TENSOR),
        check_vma=False,
    )
```

time: 225 us -> 187 us (0.83)
  the two profiles are of different devices: /device:TPU:6 before, /device:TPU:16 now
where the time goes in v2:
time: 187 us; the launch traced here: 186 us
  starting transfers between devices  73.2 us (39%)
  waiting for transfers between devices  43.2 us (23%)
  blocking collectives  41.5 us (22%)
  matrix products  8.46 us (5%)
  Pallas kernels  8.25 us (4%)
  local copies, waits for them, and re-layouts  6.93 us (4%)
  other arithmetic  4.11 us (2%)
    all_to_all x1, blocking collectives, local(): lax.all_to_all(partial_grad.astype(bf16).reshape(n_z, ds // groups, width...  41.5 us
    ppermute x8, starting transfers between devices, meet(): lax.ppermute(value, axis, [(i, i ^ bit) for i in range(lax.axis_size(axis...  31 us
    ppermute x8, waiting for transfers between devices, meet(): lax.ppermute(value, axis, [(i, i ^ bit) for i in range(lax.axis_size(axis...  23.6 us
    ppermute x6, starting transfers between devices, shift(): lax.ppermute(value, axis, [(i, (i + step) % size) for i in range(size)])  21.7 us
    ppermute x6, waiting for transfers between devices, shift(): lax.ppermute(value, axis, [(i, (i + step) % size) for i in range(size)])  16.4 us
    all_to_all x1, starting transfers between devices, local(): lax.all_to_all(packed.reshape(groups, PAD, width), DP, 0, 0, tiled=True)  16.1 us
    pallas_call x2, Pallas kernels, half_product(): pl.pallas_call(product_kernel, in_specs=[pl.BlockSpec(memory_space=pltpu....  8.25 us
    all_to_all x1, starting transfers between devices, local(): summed = lax.all_to_all(summed, 'x', 0, 0, tiled=True)  4.3 us
  transfers between devices with their start and end apart: 16, of which 6 were waited for; matrix products, arithmetic and copies ran while one was open for 7% of the time, Pallas kernels for 2%

profile of v2, /device:TPU:16, one launch (start us, length us, event | category | flops | bytes accessed | tf_op | source)
XLA Modules:
  0.0 186.0 jit_solution(2987666180758401698)
XLA Ops:
  0.0 0.9 pad.4
  0.9 0.2 reshape.143
  1.2 0.2 reshape.144
  1.4 5.9 %collective-permute-start.1 = (bf16[16,3072]{1,0:T(8,128)(2,1)S(1)}, bf16[16,3072]{1,0:T(8,128)(2,1)S(1)}, u32[]{:S(2)}, u32[]{:S(2)}) collective-permute-start(bf16[16,3072]{1,0:T(8,128)(2,1)S(1)} %reshape.144), channel_id=1, source_target_pairs={{0,2},{2,0},{1,3},{3,1},{4,6},{6,4},{5,7},{7,5},{8,10},{10,8},{9,1... | collective-permute-start | bytes 294920 | tf_op jit(solution)/shard_map/ppermute | solution.py:17
  7.4 0.9 copy-done
  8.3 3.0 %shard_map.64 = bf16[8,128,512]{2,1,0:T(8,128)(2,1)S(1)} custom-call(s32[1]{0:T(128)} %bitcast.1.core_ref, bf16[128,512]{1,0:T(8,128)(2,1)S(1)} %copy-done, bf16[512,8192]{1,0:T(8,128)(2,1)} %weight_ref.3), custom_call_target="tpu_custom_call" | custom-call | flops 536870912 | bytes 5242880 | tf_op jit(solution)/shard_map/pallas_call | solution.py:59
  11.3 1.9 %collective-permute-start = (bf16[8,128,512]{2,1,0:T(8,128)(2,1)S(1)}, bf16[8,128,512]{2,1,0:T(8,128)(2,1)S(1)}, u32[]{:S(2)}, u32[]{:S(2)}) collective-permute-start(bf16[8,128,512]{2,1,0:T(8,128)(2,1)S(1)} %shard_map.64), channel_id=1, source_target_pairs={{0,1},{1,0},{2,3},{3,2},{4,5},{5,4},{6,7},{7,6},{8,9},{9,8},{10,11... | collective-permute-start | bytes 3145736 | tf_op jit(solution)/shard_map/ppermute | solution.py:17
  13.3 0.1 convert_reduce_fusion.3
  13.4 0.2 convert_reduce_fusion.2
  13.7 2.1 %collective-permute-done.refs_0_ = bf16[8,128,512]{2,1,0:T(8,128)(2,1)S(1)} collective-permute-done((bf16[8,128,512]{2,1,0:T(8,128)(2,1)S(1)}, bf16[8,128,512]{2,1,0:T(8,128)(2,1)S(1)}, u32[]{:S(2)}, u32[]{:S(2)}) %collective-permute-start) | collective-permute-done | bytes 1048608 | tf_op jit(solution)/shard_map/ppermute | solution.py:17
  15.9 1.0 copy-done.6
  16.8 5.2 %shard_map.65 = bf16[8,128,512]{2,1,0:T(8,128)(2,1)} custom-call(s32[1]{0:T(128)} %bitcast.core_ref, bf16[128,512]{1,0:T(8,128)(2,1)S(1)} %copy-done.1, bf16[512,8192]{1,0:T(8,128)(2,1)} %weight_ref.3, bf16[8,128,512]{2,1,0:T(8,128)(2,1)} %copy-done.6), custom_call_target="tpu_custom_call" | custom-call | flops 536870912 | bytes 5242880 | tf_op jit(solution)/shard_map/pallas_call | solution.py:59
  22.1 4.3 %all-to-all-start = ((bf16[4,256,512]{2,1,0:T(8,128)(2,1)}), bf16[4,256,512]{2,1,0:T(8,128)(2,1)S(1)}, u32[]{:S(2)}, u32[]{:S(2)}) async-start(bf16[4,256,512]{2,1,0:T(8,128)(2,1)} %bitcast.7), calls=%async_computation | async-start | bytes 2097152 | tf_op jit(solution)/shard_map/all_to_all | solution.py:136
  26.4 3.9 %collective-permute-start.2 = (bf16[32,3072]{1,0:T(8,128)(2,1)S(1)}, bf16[32,3072]{1,0:T(8,128)(2,1)S(1)}, u32[]{:S(2)}, u32[]{:S(2)}) collective-permute-start(bf16[32,3072]{1,0:T(8,128)(2,1)S(1)} %pad_maximum_fusion.3), channel_id=1, source_target_pairs={{0,4},{4,0},{8,12},{12,8},{1,5},{5,1},{9,13},{13,9},{2,6},{6,2},{1... | collective-permute-start | bytes 589832 | tf_op jit(solution)/shard_map/ppermute | solution.py:17
  30.3 14.2 %collective-permute-done.2 = bf16[32,3072]{1,0:T(8,128)(2,1)S(1)} collective-permute-done((bf16[32,3072]{1,0:T(8,128)(2,1)S(1)}, bf16[32,3072]{1,0:T(8,128)(2,1)S(1)}, u32[]{:S(2)}, u32[]{:S(2)}) %collective-permute-start.2) | collective-permute-done | bytes 196640 | tf_op jit(solution)/shard_map/ppermute | solution.py:17
  44.6 3.3 %collective-permute-start.5 = (bf16[64,768]{1,0:T(8,128)(2,1)S(1)}, bf16[64,768]{1,0:T(8,128)(2,1)S(1)}, u32[]{:S(2)}, u32[]{:S(2)}) collective-permute-start(bf16[64,768]{1,0:T(8,128)(2,1)S(1)} %get-tuple-element.26), channel_id=1, source_target_pairs={{0,48},{16,0},{32,16},{48,32},{1,49},{17,1},{33,17},{49,33},{2,50}... | collective-permute-start | bytes 294920 | tf_op jit(solution)/shard_map/ppermute | solution.py:26
  47.8 5.4 %collective-permute-start.4 = (bf16[64,768]{1,0:T(8,128)(2,1)S(1)}, bf16[64,768]{1,0:T(8,128)(2,1)S(1)}, u32[]{:S(2)}, u32[]{:S(2)}) collective-permute-start(bf16[64,768]{1,0:T(8,128)(2,1)S(1)} %get-tuple-element.27), channel_id=1, source_target_pairs={{0,32},{16,48},{32,0},{48,16},{1,33},{17,49},{33,1},{49,17},{2,34}... | collective-permute-start | bytes 294920 | tf_op jit(solution)/shard_map/ppermute | solution.py:26
  53.2 3.9 %collective-permute-start.3 = (bf16[64,768]{1,0:T(8,128)(2,1)S(1)}, bf16[64,768]{1,0:T(8,128)(2,1)S(1)}, u32[]{:S(2)}, u32[]{:S(2)}) collective-permute-start(bf16[64,768]{1,0:T(8,128)(2,1)S(1)} %get-tuple-element.28), channel_id=1, source_target_pairs={{0,16},{16,32},{32,48},{48,0},{1,17},{17,33},{33,49},{49,1},{2,18}... | collective-permute-start | bytes 294920 | tf_op jit(solution)/shard_map/ppermute | solution.py:26
  57.1 0.1 convert_reduce_fusion
  57.3 0.8 copy-done.3
  58.1 0.7 fusion.32
  58.8 4.6 %collective-permute-start.7 = (bf16[64,3072]{1,0:T(8,128)(2,1)S(1)}, bf16[64,3072]{1,0:T(8,128)(2,1)}, u32[]{:S(2)}, u32[]{:S(2)}) collective-permute-start(bf16[64,3072]{1,0:T(8,128)(2,1)S(1)} %constant_dynamic-update-slice_fusion), channel_id=1, source_target_pairs={{0,8},{4,12},{8,0},{12,4},{1,9},{5,13},{9,1},{13,5},{2,10},{6,14},... | collective-permute-start | bytes 1179656 | tf_op jit(solution)/shard_map/ppermute | solution.py:17
  63.4 0.1 reshape.152
  63.5 0.8 pad_maximum_fusion.2
  64.3 8.1 %collective-permute-start.6 = (bf16[128,512]{1,0:T(8,128)(2,1)}, bf16[128,512]{1,0:T(8,128)(2,1)S(1)}, u32[]{:S(2)}, u32[]{:S(2)}) collective-permute-start(bf16[128,512]{1,0:T(8,128)(2,1)} %fusion.32), channel_id=1, source_target_pairs={{0,2},{2,0},{1,3},{3,1},{4,6},{6,4},{5,7},{7,5},{8,10},{10,8},{9,1... | collective-permute-start | bytes 393224 | tf_op jit(solution)/shard_map/ppermute | solution.py:17
  72.4 2.0 %pad_maximum_fusion = bf16[128,3072]{1,0:T(8,128)(2,1)} fusion(bf16[64,3072]{1,0:T(8,128)(2,1)} %collective-permute-done.7, bf16[64,3072]{1,0:T(8,128)(2,1)S(1)} %constant_dynamic-update-slice_fusion), kind=kLoop, calls=%fused_computation.12 | loop fusion | flops 1572864 | bytes 1572864 | tf_op jit(solution)/shard_map/concatenate | solution.py:21
  74.3 2.7 %collective-permute-done.6 = bf16[128,512]{1,0:T(8,128)(2,1)S(1)} collective-permute-done((bf16[128,512]{1,0:T(8,128)(2,1)}, bf16[128,512]{1,0:T(8,128)(2,1)S(1)}, u32[]{:S(2)}, u32[]{:S(2)}) %collective-permute-start.6) | collective-permute-done | bytes 131104 | tf_op jit(solution)/shard_map/ppermute | solution.py:17
  77.1 1.9 %convolution_convert_fusion = bf16[384,512]{1,0:T(8,128)(2,1)} fusion(bf16[128,512]{1,0:T(8,128)(2,1)S(1)} %collective-permute-done.6, f32[2,128,512]{2,1,0:T(8,128)S(1)} %bitcast.45, s32[]{:T(128)S(6)} %select_n.113, bf16[128,512]{1,0:T(8,128)(2,1)} %param.6, s32[128]{0:T(128)S(1)} %fusion.43), kind=kOutput, calls=%fused_computation.7 | convolution fusion | flops 50905088 | bytes 918020 | tf_op jit(solution)/shard_map/dot_general | solution.py:146
  79.0 16.1 %all-to-all-start.1 = ((bf16[48,8,512]{2,1,0:T(8,128)(2,1)}), bf16[48,8,512]{2,1,0:T(8,128)(2,1)}, u32[]{:S(2)}, u32[]{:S(2)}) async-start(bf16[48,8,512]{2,1,0:T(8,128)(2,1)} %bitcast.11), calls=%async_computation.1 | async-start | bytes 786432 | tf_op jit(solution)/shard_map/all_to_all | solution.py:150
  95.1 2.8 %collective-permute-start.8 = (bf16[64,3072]{1,0:T(8,128)(2,1)}, bf16[64,3072]{1,0:T(8,128)(2,1)S(1)}, u32[]{:S(2)}, u32[]{:S(2)}) collective-permute-start(bf16[64,3072]{1,0:T(8,128)(2,1)} %pad_maximum_fusion.2), channel_id=1, source_target_pairs={{0,8},{4,12},{8,0},{12,4},{1,9},{5,13},{9,1},{13,5},{2,10},{6,14},... | collective-permute-start | bytes 1179656 | tf_op jit(solution)/shard_map/ppermute | solution.py:17
  97.9 0.2 fusion.27
  98.2 1.9 %copy.11 = bf16[4,12,64,512]{3,2,1,0:T(8,128)(2,1)} copy(bf16[4,12,64,512]{3,2,0,1:T(8,128)(2,1)S(1)} %bitcast.42) | data formatting | bytes 6291456 | tf_op jit(solution)/shard_map/transpose | solution.py:134
  100.0 1.9 %collective-permute-start.10 = (bf16[128,3072]{1,0:T(8,128)(2,1)}, bf16[128,3072]{1,0:T(8,128)(2,1)}, u32[]{:S(2)}, u32[]{:S(2)}) collective-permute-start(bf16[128,3072]{1,0:T(8,128)(2,1)} %pad_maximum_fusion), channel_id=1, source_target_pairs={{0,1},{1,0},{2,3},{3,2},{4,5},{5,4},{6,7},{7,6},{8,9},{9,8},{10,11... | collective-permute-start | bytes 2359304 | tf_op jit(solution)/shard_map/ppermute | solution.py:17
  102.0 4.5 %collective-permute-done.8 = bf16[64,3072]{1,0:T(8,128)(2,1)S(1)} collective-permute-done((bf16[64,3072]{1,0:T(8,128)(2,1)}, bf16[64,3072]{1,0:T(8,128)(2,1)S(1)}, u32[]{:S(2)}, u32[]{:S(2)}) %collective-permute-start.8) | collective-permute-done | bytes 393248 | tf_op jit(solution)/shard_map/ppermute | solution.py:17
  106.6 1.9 %collective-permute-start.9 = (bf16[128,3072]{1,0:T(8,128)(2,1)S(1)}, bf16[128,3072]{1,0:T(8,128)(2,1)S(1)}, u32[]{:S(2)}, u32[]{:S(2)}) collective-permute-start(bf16[128,3072]{1,0:T(8,128)(2,1)S(1)} %pad_maximum_fusion.1), channel_id=1, source_target_pairs={{0,1},{1,0},{2,3},{3,2},{4,5},{5,4},{6,7},{7,6},{8,9},{9,8},{10,11... | collective-permute-start | bytes 2359304 | tf_op jit(solution)/shard_map/ppermute | solution.py:17
  108.6 3.2 %all-to-all-done.1 = bf16[48,8,512]{2,1,0:T(8,128)(2,1)} async-done(((bf16[48,8,512]{2,1,0:T(8,128)(2,1)}), bf16[48,8,512]{2,1,0:T(8,128)(2,1)}, u32[]{:S(2)}, u32[]{:S(2)}) %all-to-all-start.1) | async-done | bytes 393248 | tf_op jit(solution)/shard_map/all_to_all | solution.py:150
  111.8 1.3 fusion.26
  113.1 3.4 %fusion.13 = bf16[256,512]{1,0:T(8,128)(2,1)S(1)} fusion(f32[256,512]{1,0:T(8,128)S(1)} %fusion.26, bf16[3072,512]{1,0:T(8,128)(2,1)} %bitcast.43, bf16[128,3072]{1,0:T(8,128)(2,1)} %collective-permute-done.10, bf16[128,3072]{1,0:T(8,128)(2,1)} %pad_maximum_fusion, pred[256]{0:T(512)(128)(4,1)S(1)} %broadcast_compare_fusion), kind=kOutput, calls=%fused_computation.11 | convolution fusion | flops 808976384 | bytes 5505280 | tf_op jit(solution)/shard_map/dot_general | solution.py:149
  116.5 2.8 %collective-permute-start.13 = (bf16[256,512]{1,0:T(8,128)(2,1)S(1)}, bf16[256,512]{1,0:T(8,128)(2,1)S(1)}, u32[]{:S(2)}, u32[]{:S(2)}) collective-permute-start(bf16[256,512]{1,0:T(8,128)(2,1)S(1)} %fusion.13), channel_id=1, source_target_pairs={{0,48},{16,0},{32,16},{48,32},{1,49},{17,1},{33,17},{49,33},{2,50}... | collective-permute-start | bytes 786440 | tf_op jit(solution)/shard_map/ppermute | solution.py:26
  119.4 2.9 %collective-permute-start.12 = (bf16[256,512]{1,0:T(8,128)(2,1)S(1)}, bf16[256,512]{1,0:T(8,128)(2,1)S(1)}, u32[]{:S(2)}, u32[]{:S(2)}) collective-permute-start(bf16[256,512]{1,0:T(8,128)(2,1)S(1)} %fusion.13), channel_id=1, source_target_pairs={{0,32},{16,48},{32,0},{48,16},{1,33},{17,49},{33,1},{49,17},{2,34}... | collective-permute-start | bytes 786440 | tf_op jit(solution)/shard_map/ppermute | solution.py:26
  122.3 3.4 %collective-permute-start.11 = (bf16[256,512]{1,0:T(8,128)(2,1)S(1)}, bf16[256,512]{1,0:T(8,128)(2,1)S(1)}, u32[]{:S(2)}, u32[]{:S(2)}) collective-permute-start(bf16[256,512]{1,0:T(8,128)(2,1)S(1)} %fusion.13), channel_id=1, source_target_pairs={{0,16},{16,32},{32,48},{48,0},{1,17},{17,33},{33,49},{49,1},{2,18}... | collective-permute-start | bytes 786440 | tf_op jit(solution)/shard_map/ppermute | solution.py:26
  125.8 0.4 fusion.24
  126.2 16.4 %collective-permute-done.11 = bf16[256,512]{1,0:T(8,128)(2,1)S(1)} collective-permute-done((bf16[256,512]{1,0:T(8,128)(2,1)S(1)}, bf16[256,512]{1,0:T(8,128)(2,1)S(1)}, u32[]{:S(2)}, u32[]{:S(2)}) %collective-permute-start.11) | collective-permute-done | bytes 262176 | tf_op jit(solution)/shard_map/ppermute | solution.py:26
  142.6 0.4 fusion.22
  143.0 0.4 fusion.20
  143.4 0.4 add_convert_fusion
  143.8 41.5 %all_to_all.15 = bf16[12,64,512]{2,1,0:T(8,128)(2,1)S(1)} all-to-all(bf16[12,64,512]{2,1,0:T(8,128)(2,1)S(1)} %bitcast.41), channel_id=1, replica_groups=mesh['z'=12,'yl'=4,'x'=4,'yh'=2,'core'=2] {'z'}, dimensions={0} | all-to-all | bytes 1572864 | tf_op jit(solution)/shard_map/all_to_all | solution.py:167
  185.3 0.8 convert_reduce_fusion.1
  (36 shorter events, 0.5 us)
Async XLA Ops:
  1.4 12.3 %collective-permute-start.1 = (bf16[16,3072]{1,0:T(8,128)(2,1)S(1)}, bf16[16,3072]{1,0:T(8,128)(2,1)S(1)}, u32[]{:S(2)}, u32[]{:S(2)}) collective-permute-start(bf16[16,3072]{1,0:T(8,128)(2,1)S(1)} %reshape.144), channel_id=1, source_target_pairs={{0,2},{2,0},{1,3},{3,1},{4,6},{6,4},{5,7},{7,5},{8,10},{10,8},{9,1... | collective-permute-start | bytes 294920 | tf_op jit(solution)/shard_map/ppermute | solution.py:17
  7.4 0.9 copy-start
  8.3 5.0 %copy-start.7 = (s32[6144,1]{0,1:T(1,128)S(1)}, s32[6144,1]{0,1:T(1,128)}, u32[]{:S(2)}) copy-start(s32[6144,1]{0,1:T(1,128)} %param.11) | copy-start | bytes 73732
  8.3 8.6 %copy-start.1 = (bf16[128,512]{1,0:T(8,128)(2,1)S(1)}, bf16[128,512]{1,0:T(8,128)(2,1)}, u32[]{:S(2)}) copy-start(bf16[128,512]{1,0:T(8,128)(2,1)} %rows_ref.3) | copy-start | bytes 393220
  11.3 4.6 %collective-permute-start = (bf16[8,128,512]{2,1,0:T(8,128)(2,1)S(1)}, bf16[8,128,512]{2,1,0:T(8,128)(2,1)S(1)}, u32[]{:S(2)}, u32[]{:S(2)}) collective-permute-start(bf16[8,128,512]{2,1,0:T(8,128)(2,1)S(1)} %shard_map.64), channel_id=1, source_target_pairs={{0,1},{1,0},{2,3},{3,2},{4,5},{5,4},{6,7},{7,6},{8,9},{9,8},{10,11... | collective-permute-start | bytes 3145736 | tf_op jit(solution)/shard_map/ppermute | solution.py:17
  15.9 1.0 copy-start.6
  22.1 35.1 %all-to-all-start = ((bf16[4,256,512]{2,1,0:T(8,128)(2,1)}), bf16[4,256,512]{2,1,0:T(8,128)(2,1)S(1)}, u32[]{:S(2)}, u32[]{:S(2)}) async-start(bf16[4,256,512]{2,1,0:T(8,128)(2,1)} %bitcast.7), calls=%async_computation | async-start | bytes 2097152 | tf_op jit(solution)/shard_map/all_to_all | solution.py:136
  26.4 18.1 %collective-permute-start.2 = (bf16[32,3072]{1,0:T(8,128)(2,1)S(1)}, bf16[32,3072]{1,0:T(8,128)(2,1)S(1)}, u32[]{:S(2)}, u32[]{:S(2)}) collective-permute-start(bf16[32,3072]{1,0:T(8,128)(2,1)S(1)} %pad_maximum_fusion.3), channel_id=1, source_target_pairs={{0,4},{4,0},{8,12},{12,8},{1,5},{5,1},{9,13},{13,9},{2,6},{6,2},{1... | collective-permute-start | bytes 589832 | tf_op jit(solution)/shard_map/ppermute | solution.py:17
  44.6 18.9 %collective-permute-start.5 = (bf16[64,768]{1,0:T(8,128)(2,1)S(1)}, bf16[64,768]{1,0:T(8,128)(2,1)S(1)}, u32[]{:S(2)}, u32[]{:S(2)}) collective-permute-start(bf16[64,768]{1,0:T(8,128)(2,1)S(1)} %get-tuple-element.26), channel_id=1, source_target_pairs={{0,48},{16,0},{32,16},{48,32},{1,49},{17,1},{33,17},{49,33},{2,50}... | collective-permute-start | bytes 294920 | tf_op jit(solution)/shard_map/ppermute | solution.py:26
  47.8 15.7 %collective-permute-start.4 = (bf16[64,768]{1,0:T(8,128)(2,1)S(1)}, bf16[64,768]{1,0:T(8,128)(2,1)S(1)}, u32[]{:S(2)}, u32[]{:S(2)}) collective-permute-start(bf16[64,768]{1,0:T(8,128)(2,1)S(1)} %get-tuple-element.27), channel_id=1, source_target_pairs={{0,32},{16,48},{32,0},{48,16},{1,33},{17,49},{33,1},{49,17},{2,34}... | collective-permute-start | bytes 294920 | tf_op jit(solution)/shard_map/ppermute | solution.py:26
  53.2 10.3 %collective-permute-start.3 = (bf16[64,768]{1,0:T(8,128)(2,1)S(1)}, bf16[64,768]{1,0:T(8,128)(2,1)S(1)}, u32[]{:S(2)}, u32[]{:S(2)}) collective-permute-start(bf16[64,768]{1,0:T(8,128)(2,1)S(1)} %get-tuple-element.28), channel_id=1, source_target_pairs={{0,16},{16,32},{32,48},{48,0},{1,17},{17,33},{33,49},{49,1},{2,18}... | collective-permute-start | bytes 294920 | tf_op jit(solution)/shard_map/ppermute | solution.py:26
  57.3 0.8 copy-start.3
  58.8 13.6 %collective-permute-start.7 = (bf16[64,3072]{1,0:T(8,128)(2,1)S(1)}, bf16[64,3072]{1,0:T(8,128)(2,1)}, u32[]{:S(2)}, u32[]{:S(2)}) collective-permute-start(bf16[64,3072]{1,0:T(8,128)(2,1)S(1)} %constant_dynamic-update-slice_fusion), channel_id=1, source_target_pairs={{0,8},{4,12},{8,0},{12,4},{1,9},{5,13},{9,1},{13,5},{2,10},{6,14},... | collective-permute-start | bytes 1179656 | tf_op jit(solution)/shard_map/ppermute | solution.py:17
  63.5 13.6 %copy-start.4 = (f32[256,512]{1,0:T(8,128)S(1)}, f32[256,512]{1,0:T(8,128)}, u32[]{:S(2)}) copy-start(f32[256,512]{1,0:T(8,128)} %copy-done.3) | copy-start | bytes 1572868
  64.3 33.9 %copy-start.2 = (bf16[3072,512]{1,0:T(8,128)(2,1)S(1)}, bf16[3072,512]{1,0:T(8,128)(2,1)}, u32[]{:S(2)}) copy-start(bf16[3072,512]{1,0:T(8,128)(2,1)} %param.9) | copy-start | bytes 9437188
  64.3 12.8 %collective-permute-start.6 = (bf16[128,512]{1,0:T(8,128)(2,1)}, bf16[128,512]{1,0:T(8,128)(2,1)S(1)}, u32[]{:S(2)}, u32[]{:S(2)}) collective-permute-start(bf16[128,512]{1,0:T(8,128)(2,1)} %fusion.32), channel_id=1, source_target_pairs={{0,2},{2,0},{1,3},{3,1},{4,6},{6,4},{5,7},{7,5},{8,10},{10,8},{9,1... | collective-permute-start | bytes 393224 | tf_op jit(solution)/shard_map/ppermute | solution.py:17
  79.0 32.8 %all-to-all-start.1 = ((bf16[48,8,512]{2,1,0:T(8,128)(2,1)}), bf16[48,8,512]{2,1,0:T(8,128)(2,1)}, u32[]{:S(2)}, u32[]{:S(2)}) async-start(bf16[48,8,512]{2,1,0:T(8,128)(2,1)} %bitcast.11), calls=%async_computation.1 | async-start | bytes 786432 | tf_op jit(solution)/shard_map/all_to_all | solution.py:150
  95.1 11.4 %collective-permute-start.8 = (bf16[64,3072]{1,0:T(8,128)(2,1)}, bf16[64,3072]{1,0:T(8,128)(2,1)S(1)}, u32[]{:S(2)}, u32[]{:S(2)}) collective-permute-start(bf16[64,3072]{1,0:T(8,128)(2,1)} %pad_maximum_fusion.2), channel_id=1, source_target_pairs={{0,8},{4,12},{8,0},{12,4},{1,9},{5,13},{9,1},{13,5},{2,10},{6,14},... | collective-permute-start | bytes 1179656 | tf_op jit(solution)/shard_map/ppermute | solution.py:17
  98.2 8.3 %copy-start.5 = (bf16[64,3072]{1,0:T(8,128)(2,1)S(1)}, bf16[64,3072]{1,0:T(8,128)(2,1)}, u32[]{:S(2)}) copy-start(bf16[64,3072]{1,0:T(8,128)(2,1)} %pad_maximum_fusion.2) | copy-start | bytes 1179652
  100.0 13.1 %collective-permute-start.10 = (bf16[128,3072]{1,0:T(8,128)(2,1)}, bf16[128,3072]{1,0:T(8,128)(2,1)}, u32[]{:S(2)}, u32[]{:S(2)}) collective-permute-start(bf16[128,3072]{1,0:T(8,128)(2,1)} %pad_maximum_fusion), channel_id=1, source_target_pairs={{0,1},{1,0},{2,3},{3,2},{4,5},{5,4},{6,7},{7,6},{8,9},{9,8},{10,11... | collective-permute-start | bytes 2359304 | tf_op jit(solution)/shard_map/ppermute | solution.py:17
  106.6 19.1 %collective-permute-start.9 = (bf16[128,3072]{1,0:T(8,128)(2,1)S(1)}, bf16[128,3072]{1,0:T(8,128)(2,1)S(1)}, u32[]{:S(2)}, u32[]{:S(2)}) collective-permute-start(bf16[128,3072]{1,0:T(8,128)(2,1)S(1)} %pad_maximum_fusion.1), channel_id=1, source_target_pairs={{0,1},{1,0},{2,3},{3,2},{4,5},{5,4},{6,7},{7,6},{8,9},{9,8},{10,11... | collective-permute-start | bytes 2359304 | tf_op jit(solution)/shard_map/ppermute | solution.py:17
  116.5 26.9 %collective-permute-start.13 = (bf16[256,512]{1,0:T(8,128)(2,1)S(1)}, bf16[256,512]{1,0:T(8,128)(2,1)S(1)}, u32[]{:S(2)}, u32[]{:S(2)}) collective-permute-start(bf16[256,512]{1,0:T(8,128)(2,1)S(1)} %fusion.13), channel_id=1, source_target_pairs={{0,48},{16,0},{32,16},{48,32},{1,49},{17,1},{33,17},{49,33},{2,50}... | collective-permute-start | bytes 786440 | tf_op jit(solution)/shard_map/ppermute | solution.py:26
  119.4 23.6 %collective-permute-start.12 = (bf16[256,512]{1,0:T(8,128)(2,1)S(1)}, bf16[256,512]{1,0:T(8,128)(2,1)S(1)}, u32[]{:S(2)}, u32[]{:S(2)}) collective-permute-start(bf16[256,512]{1,0:T(8,128)(2,1)S(1)} %fusion.13), channel_id=1, source_target_pairs={{0,32},{16,48},{32,0},{48,16},{1,33},{17,49},{33,1},{49,17},{2,34}... | collective-permute-start | bytes 786440 | tf_op jit(solution)/shard_map/ppermute | solution.py:26
  122.3 20.3 %collective-permute-start.11 = (bf16[256,512]{1,0:T(8,128)(2,1)S(1)}, bf16[256,512]{1,0:T(8,128)(2,1)S(1)}, u32[]{:S(2)}, u32[]{:S(2)}) collective-permute-start(bf16[256,512]{1,0:T(8,128)(2,1)S(1)} %fusion.13), channel_id=1, source_target_pairs={{0,16},{16,32},{32,48},{48,0},{1,17},{17,33},{33,49},{49,1},{2,18}... | collective-permute-start | bytes 786440 | tf_op jit(solution)/shard_map/ppermute | solution.py:26

commit v3 on v2

--- a/solution.py
+++ b/solution.py
@@ -18,7 +18,7 @@
 
 
 def joined(value, axis, bit):
-    return jnp.concatenate([value, meet(value, axis, bit)], axis=0)
+    return jnp.concatenate([value, meet(value, axis, bit)], axis=1)
 
 
 def shift(value, axis, step):
@@ -85,8 +85,7 @@
     groups = n_z * n_yl
     n_t = n_x * n_yh * n_c
     my_group = lax.axis_index(DP)
-    my_yl, my_x = lax.axis_index("yl"), lax.axis_index("x")
-    my_yh, my_core = lax.axis_index("yh"), lax.axis_index("core")
+    my_x, my_yh, my_core = (lax.axis_index(axis) for axis in TENSOR)
     rows, width = attn_out.shape
     own, ds = student_in.shape
     cap = own * n_t // groups
@@ -97,18 +96,22 @@
     given = half_product(attn_out, w_out, 1 - my_core, n_x * n_yh)
     taken = meet(given, "core", 1)
 
-    whole = jnp.pad(student_in, ((0, 1), (0, 0)))
-    whole = whole.reshape(slots, n_z, n_yl, ds // groups).transpose(0, 2, 1, 3).reshape(slots, ds)
-    whole = joined(whole, "yh", 1)
+    block = jnp.pad(student_in, ((0, 1), (0, 0)))
+    block = block.reshape(slots, n_z, n_yl, ds // groups).transpose(2, 0, 1, 3)
+    block = block.reshape(n_yl, slots, part)
+    block = jnp.concatenate([block, lax.all_to_all(block, "yl", 0, 0, tiled=True)], axis=0)
+    block = joined(block, "yh", 1)
 
-    slot = jnp.arange(n_t * slots, dtype=jnp.int32)
-    place, order = slot % slots, slot // slots
+    slot = jnp.arange(n_t * own, dtype=jnp.int32)
+    place, order = slot % own, slot // own
     from_yh = my_yh ^ (order % n_yh)
-    from_x = my_x ^ (order // n_yh % n_x)
+    from_x = (my_x + n_x - order // n_yh % n_x) % n_x
     from_core = my_core ^ (order // (n_yh * n_x))
     holder = (from_x * n_yh + from_yh) * n_c + from_core
-    origin = jnp.where(place < own, (holder * per + place // cap) * PAD + place % cap, -1)
+    origin = (holder * per + place // cap) * PAD + place % cap
     placing = (origin[:, None] == jnp.arange(groups * PAD, dtype=jnp.int32)[None, :]).astype(bf16)
+    kept_rows = order * slots + place
+    closing = (kept_rows[:, None] == jnp.arange(n_t * slots, dtype=jnp.int32)[None, :]).astype(bf16)
     dest_table = dest[:, 0].reshape(groups, rows)
     counts = jnp.sum((dest_table == my_group).astype(jnp.int32), axis=1)
     filled = (jnp.arange(PAD, dtype=jnp.int32)[None, :] < counts[:, None]).reshape(groups * PAD)
@@ -123,44 +126,38 @@
     ).astype(bf16)
 
     summed = half_product(attn_out, w_out, my_core, n_x * n_yh, taken)
-    summed, whole = lax.optimization_barrier((summed, whole))
-    whole = joined(whole, "x", 1)
-
-    def lanes(k):
-        first = lax.rem(my_yl + k, n_yl) * part
-        return lax.dynamic_slice_in_dim(whole, first, part, 1)
-
-    quarter = [lanes(0)] + [shift(lanes(k), "yl", k) for k in range(1, n_yl)]
-    weight = after(proj, whole).reshape(n_z, n_yl, ds // groups, width).transpose(1, 0, 2, 3)
+    block = after(block, summed)
+    block = jnp.concatenate([block] + [shift(block, "x", k) for k in range(1, n_x)], axis=1)
+    weight = proj.reshape(n_z, n_yl, ds // groups, width).transpose(1, 0, 2, 3)
+    weight = weight.reshape(n_yl, part, width)
     summed = summed.reshape(n_x, n_yh * rows, width)
     summed = lax.all_to_all(summed, "x", 0, 0, tiled=True)
     summed = jnp.sum(summed.astype(f32), axis=0).reshape(n_yh, rows, width)
     given = pick(summed, 1 - my_yh).astype(bf16)
     kept = resid.astype(f32) + pick(summed, my_yh)
-    given, whole = lax.optimization_barrier((given, whole))
     taken = meet(given, "yh", 1)
-    whole = joined(whole, "x", 2)
-    taken, whole = lax.optimization_barrier((taken, whole))
+    taken, block, weight = lax.optimization_barrier((taken, block, weight))
     hidden = (kept + taken.astype(f32)).astype(bf16)
 
     packed = jnp.dot(selector, hidden, preferred_element_type=f32).astype(bf16)
-    quarter = joined(after(jnp.concatenate(quarter, axis=1), packed), "x", 2)
-    whole = joined(after(whole, packed), "core", 1)
-    predicted = jnp.dot(whole, weight.reshape(ds, width), preferred_element_type=f32)
+    block = joined(after(block, packed), "core", 1)
+    parts = lax.optimization_barrier(
+        [jnp.dot(closing, rows16, preferred_element_type=f32).astype(bf16) for rows16 in block]
+    )
+    predicted = sum(
+        jnp.dot(parts[k], weight[k], preferred_element_type=f32) for k in range(n_yl)
+    )
     arrived = lax.all_to_all(
         packed.reshape(groups, PAD, width), DP, 0, 0, tiled=True
     ).reshape(groups * PAD, width)
     targets = jnp.dot(placing, arrived, preferred_element_type=f32)
     mismatch = (jnp.where(valid, predicted - targets, 0.0) / rows).astype(bf16)
 
-    quarter = joined(after(quarter, arrived), "core", 1)
-    mismatches = [mismatch] + [shift(mismatch, "yl", k) for k in range(1, n_yl)]
+    mismatch = lax.all_gather(mismatch, "yl", axis=0, tiled=True)
+    mismatch = mismatch.reshape(n_yl, n_t * own, width)
     partial_grad = sum(
         lax.dot_general(
-            quarter[:, k * part : (k + 1) * part],
-            mismatches[k],
-            (((0,), (0,)), ((), ())),
-            preferred_element_type=f32,
+            parts[n_yl + k], mismatch[k], (((0,), (0,)), ((), ())), preferred_element_type=f32
         )
         for k in range(n_yl)
     )

time: 187 us -> 172 us (0.920)
  the two profiles are of different devices: /device:TPU:16 before, /device:TPU:6 now
where the time goes in v3:
time: 172 us; the launch traced here: 169 us
  blocking collectives  53.7 us (31%)
  starting transfers between devices  46.8 us (27%)
  waiting for transfers between devices  42.8 us (25%)
  Pallas kernels  8.23 us (5%)
  local copies, waits for them, and re-layouts  8.16 us (5%)
  matrix products  7.02 us (4%)
    all_to_all x1, blocking collectives, local(): lax.all_to_all(partial_grad.astype(bf16).reshape(n_z, ds // groups, width...  34.3 us
    all_gather x1, blocking collectives, local(): mismatch = lax.all_gather(mismatch, 'yl', axis=0, tiled=True)  19.4 us
    all_to_all x1, waiting for transfers between devices, local(): lax.all_to_all(packed.reshape(groups, PAD, width), DP, 0, 0, tiled=True)  17.6 us
    ppermute x4, waiting for transfers between devices, meet(): lax.ppermute(value, axis, [(i, i ^ bit) for i in range(lax.axis_size(axis...  15.6 us
    all_to_all x1, starting transfers between devices, local(): lax.all_to_all(packed.reshape(groups, PAD, width), DP, 0, 0, tiled=True)  14.1 us
    all_to_all x1, starting transfers between devices, local(): summed = lax.all_to_all(summed, 'x', 0, 0, tiled=True)  11.4 us
    ppermute x3, waiting for transfers between devices, shift(): lax.ppermute(value, axis, [(i, (i + step) % size) for i in range(size)])  9.6 us
    ppermute x3, starting transfers between devices, shift(): lax.ppermute(value, axis, [(i, (i + step) % size) for i in range(size)])  8.66 us
  transfers between devices with their start and end apart: 10, of which 6 were waited for; matrix products, arithmetic and copies ran while one was open for 7% of the time, Pallas kernels for 3%

profile of v3, /device:TPU:6, one launch (start us, length us, event | category | flops | bytes accessed | tf_op | source)
XLA Modules:
  0.0 168.5 jit_solution(11970146891993631577)
XLA Ops:
  0.0 0.9 copy-done
  0.9 3.0 %shard_map.64 = bf16[8,128,512]{2,1,0:T(8,128)(2,1)S(1)} custom-call(s32[1]{0:T(128)} %bitcast.1.core_ref, bf16[128,512]{1,0:T(8,128)(2,1)S(1)} %copy-done, bf16[512,8192]{1,0:T(8,128)(2,1)} %weight_ref.3), custom_call_target="tpu_custom_call" | custom-call | flops 536870912 | bytes 5242880 | tf_op jit(solution)/shard_map/pallas_call | solution.py:59
  3.9 1.9 %collective-permute-start = (bf16[8,128,512]{2,1,0:T(8,128)(2,1)S(1)}, bf16[8,128,512]{2,1,0:T(8,128)(2,1)S(1)}, u32[]{:S(2)}, u32[]{:S(2)}) collective-permute-start(bf16[8,128,512]{2,1,0:T(8,128)(2,1)S(1)} %shard_map.64), channel_id=1, source_target_pairs={{0,1},{1,0},{2,3},{3,2},{4,5},{5,4},{6,7},{7,6},{8,9},{9,8},{10,11... | collective-permute-start | bytes 3145736 | tf_op jit(solution)/shard_map/ppermute | solution.py:17
  5.9 0.2 reshape.164
  6.1 0.8 reshape.165
  7.0 4.9 %all-to-all-start.1 = ((bf16[4,16,768]{2,1,0:T(8,128)(2,1)}), bf16[4,16,768]{2,1,0:T(8,128)(2,1)S(1)}, u32[]{:S(2)}, u32[]{:S(2)}) async-start(bf16[4,16,768]{2,1,0:T(8,128)(2,1)} %reshape.165), calls=%async_computation.1 | async-start | bytes 196608 | tf_op jit(solution)/shard_map/all_to_all | solution.py:102
  11.8 3.9 %copy.11 = bf16[4,12,64,512]{3,2,1,0:T(8,128)(2,1)} copy(bf16[4,12,64,512]{3,2,0,1:T(8,128)(2,1)} %bitcast.85) | data formatting | bytes 6291456 | tf_op jit(solution)/shard_map/transpose | solution.py:131
  15.8 1.0 copy-done.3
  16.7 5.2 %shard_map.65 = bf16[8,128,512]{2,1,0:T(8,128)(2,1)} custom-call(s32[1]{0:T(128)} %bitcast.core_ref, bf16[128,512]{1,0:T(8,128)(2,1)S(1)} %copy-done.1, bf16[512,8192]{1,0:T(8,128)(2,1)} %weight_ref.3, bf16[8,128,512]{2,1,0:T(8,128)(2,1)} %copy-done.3), custom_call_target="tpu_custom_call" | custom-call | flops 536870912 | bytes 5242880 | tf_op jit(solution)/shard_map/pallas_call | solution.py:59
  21.9 11.4 %all-to-all-start = ((bf16[4,256,512]{2,1,0:T(8,128)(2,1)}), bf16[4,256,512]{2,1,0:T(8,128)(2,1)S(1)}, u32[]{:S(2)}, u32[]{:S(2)}) async-start(bf16[4,256,512]{2,1,0:T(8,128)(2,1)} %bitcast.2), calls=%async_computation | async-start | bytes 2097152 | tf_op jit(solution)/shard_map/all_to_all | solution.py:134
  33.4 0.9 constant_dynamic-update-slice_fusion.1
  34.3 1.9 %collective-permute-start.2 = (bf16[8,16,768]{2,1,0:T(8,128)(2,1)S(1)}, bf16[8,16,768]{2,1,0:T(8,128)(2,1)S(1)}, u32[]{:S(2)}, u32[]{:S(2)}) collective-permute-start(bf16[8,16,768]{2,1,0:T(8,128)(2,1)S(1)} %constant_dynamic-update-slice_fusion), channel_id=1, source_target_pairs={{0,2},{2,0},{1,3},{3,1},{4,6},{6,4},{5,7},{7,5},{8,10},{10,8},{9,1... | collective-permute-start | bytes 589832 | tf_op jit(solution)/shard_map/ppermute | solution.py:17
  36.3 0.2 convert_reduce_fusion.2
  36.5 14.9 %collective-permute-done.2 = bf16[8,16,768]{2,1,0:T(8,128)(2,1)S(1)} collective-permute-done((bf16[8,16,768]{2,1,0:T(8,128)(2,1)S(1)}, bf16[8,16,768]{2,1,0:T(8,128)(2,1)S(1)}, u32[]{:S(2)}, u32[]{:S(2)}) %collective-permute-start.2) | collective-permute-done | bytes 196640 | tf_op jit(solution)/shard_map/ppermute | solution.py:17
  51.4 2.2 %collective-permute-start.3 = (bf16[8,32,768]{2,1,0:T(8,128)(2,1)S(1)}, bf16[8,32,768]{2,1,0:T(8,128)(2,1)S(1)}, u32[]{:S(2)}, u32[]{:S(2)}) collective-permute-start(bf16[8,32,768]{2,1,0:T(8,128)(2,1)S(1)} %pad_maximum_fusion.1), channel_id=1, source_target_pairs={{0,4},{4,8},{8,12},{12,0},{1,5},{5,9},{9,13},{13,1},{2,6},{6,10},{... | collective-permute-start | bytes 1179656 | tf_op jit(solution)/shard_map/ppermute | solution.py:26
  53.7 4.5 %collective-permute-start.4 = (bf16[8,32,768]{2,1,0:T(8,128)(2,1)S(1)}, bf16[8,32,768]{2,1,0:T(8,128)(2,1)S(1)}, u32[]{:S(2)}, u32[]{:S(2)}) collective-permute-start(bf16[8,32,768]{2,1,0:T(8,128)(2,1)S(1)} %pad_maximum_fusion.1), channel_id=1, source_target_pairs={{0,8},{4,12},{8,0},{12,4},{1,9},{5,13},{9,1},{13,5},{2,10},{6,14},... | collective-permute-start | bytes 1179656 | tf_op jit(solution)/shard_map/ppermute | solution.py:26
  58.2 1.9 %collective-permute-start.5 = (bf16[8,32,768]{2,1,0:T(8,128)(2,1)S(1)}, bf16[8,32,768]{2,1,0:T(8,128)(2,1)S(1)}, u32[]{:S(2)}, u32[]{:S(2)}) collective-permute-start(bf16[8,32,768]{2,1,0:T(8,128)(2,1)S(1)} %pad_maximum_fusion.1), channel_id=1, source_target_pairs={{0,12},{4,0},{8,4},{12,8},{1,13},{5,1},{9,5},{13,9},{2,14},{6,2},{... | collective-permute-start | bytes 1179656 | tf_op jit(solution)/shard_map/ppermute | solution.py:26
  60.1 0.1 convert_reduce_fusion
  60.3 1.9 %collective-permute-start.1 = (bf16[128,512]{1,0:T(8,128)(2,1)S(1)}, bf16[128,512]{1,0:T(8,128)(2,1)S(1)}, u32[]{:S(2)}, u32[]{:S(2)}) collective-permute-start(bf16[128,512]{1,0:T(8,128)(2,1)S(1)} %fusion.25), channel_id=1, source_target_pairs={{0,2},{2,0},{1,3},{3,1},{4,6},{6,4},{5,7},{7,5},{8,10},{10,8},{9,1... | collective-permute-start | bytes 393224 | tf_op jit(solution)/shard_map/ppermute | solution.py:17
  62.3 1.6 collective-permute-done.3
  63.9 3.9 %collective-permute-done.4 = bf16[8,32,768]{2,1,0:T(8,128)(2,1)S(1)} collective-permute-done((bf16[8,32,768]{2,1,0:T(8,128)(2,1)S(1)}, bf16[8,32,768]{2,1,0:T(8,128)(2,1)S(1)}, u32[]{:S(2)}, u32[]{:S(2)}) %collective-permute-start.4) | collective-permute-done | bytes 393248 | tf_op jit(solution)/shard_map/ppermute | solution.py:26
  67.8 4.1 %collective-permute-done.5 = bf16[8,32,768]{2,1,0:T(8,128)(2,1)S(1)} collective-permute-done((bf16[8,32,768]{2,1,0:T(8,128)(2,1)S(1)}, bf16[8,32,768]{2,1,0:T(8,128)(2,1)S(1)}, u32[]{:S(2)}, u32[]{:S(2)}) %collective-permute-start.5) | collective-permute-done | bytes 393248 | tf_op jit(solution)/shard_map/ppermute | solution.py:26
  72.0 0.6 collective-permute-done.1
  72.6 1.0 convolution_convert_fusion
  73.7 1.9 %collective-permute-start.6 = (bf16[8,128,768]{2,1,0:T(8,128)(2,1)S(1)}, bf16[8,128,768]{2,1,0:T(8,128)(2,1)S(1)}, u32[]{:S(2)}, u32[]{:S(2)}) collective-permute-start(bf16[8,128,768]{2,1,0:T(8,128)(2,1)S(1)} %pad_maximum_fusion), channel_id=1, source_target_pairs={{0,1},{1,0},{2,3},{3,2},{4,5},{5,4},{6,7},{7,6},{8,9},{9,8},{10,11... | collective-permute-start | bytes 4718600 | tf_op jit(solution)/shard_map/ppermute | solution.py:17
  75.9 0.2 fusion.13
  76.2 14.1 %all-to-all-start.2 = ((bf16[48,8,512]{2,1,0:T(8,128)(2,1)}), bf16[48,8,512]{2,1,0:T(8,128)(2,1)S(1)}, u32[]{:S(2)}, u32[]{:S(2)}) async-start(bf16[48,8,512]{2,1,0:T(8,128)(2,1)} %bitcast.27), calls=%async_computation.2 | async-start | bytes 786432 | tf_op jit(solution)/shard_map/all_to_all | solution.py:150
  90.6 0.3 convolution_convert_fusion.1
  90.9 0.3 convolution_convert_fusion.2
  91.2 0.3 convolution_convert_fusion.3
  91.5 0.3 convolution_convert_fusion.4
  91.8 0.3 convolution_convert_fusion.5
  92.1 0.3 convolution_convert_fusion.6
  92.4 0.3 convolution_convert_fusion.7
  92.7 0.3 convolution_convert_fusion.8
  93.0 0.3 fusion.6
  93.4 0.4 convolution_add_fusion.2
  93.8 0.4 convolution_add_fusion.1
  94.1 0.4 convolution_add_fusion
  94.5 17.6 %all-to-all-done.2 = bf16[48,8,512]{2,1,0:T(8,128)(2,1)S(1)} async-done(((bf16[48,8,512]{2,1,0:T(8,128)(2,1)}), bf16[48,8,512]{2,1,0:T(8,128)(2,1)S(1)}, u32[]{:S(2)}, u32[]{:S(2)}) %all-to-all-start.2) | async-done | bytes 393248 | tf_op jit(solution)/shard_map/all_to_all | solution.py:150
  112.1 0.3 fusion.2
  112.4 19.4 %all_gather.3 = bf16[960,512]{1,0:T(8,128)(2,1)S(1)} all-gather(bf16[240,512]{1,0:T(8,128)(2,1)S(1)} %fusion.2), channel_id=1, replica_groups=mesh['z'=12,'yl'=4,'x'=4,'yh'=2,'core'=2] {'yl'}, dimensions={0}, use_global_device_ids=true | all-gather | bytes 1228800 | tf_op jit(solution)/shard_map/all_gather | solution.py:156
  131.8 0.4 fusion.19
  132.2 0.4 fusion.21
  132.6 0.4 fusion.17
  133.0 0.4 add_convert_fusion
  133.4 34.3 %all_to_all.20 = bf16[12,64,512]{2,1,0:T(8,128)(2,1)S(1)} all-to-all(bf16[12,64,512]{2,1,0:T(8,128)(2,1)S(1)} %bitcast.84), channel_id=1, replica_groups=mesh['z'=12,'yl'=4,'x'=4,'yh'=2,'core'=2] {'z'}, dimensions={0} | all-to-all | bytes 1572864 | tf_op jit(solution)/shard_map/all_to_all | solution.py:164
  167.7 0.8 convert_reduce_fusion.1
  (32 shorter events, 0.8 us)
Async XLA Ops:
  0.0 0.9 copy-start
  0.9 5.0 %copy-start.5 = (bf16[15,3072]{1,0:T(8,128)(2,1)S(1)}, bf16[15,3072]{1,0:T(8,128)(2,1)}, u32[]{:S(2)}) copy-start(bf16[15,3072]{1,0:T(8,128)(2,1)} %param.10) | copy-start | bytes 276484
  3.9 11.8 %collective-permute-start = (bf16[8,128,512]{2,1,0:T(8,128)(2,1)S(1)}, bf16[8,128,512]{2,1,0:T(8,128)(2,1)S(1)}, u32[]{:S(2)}, u32[]{:S(2)}) collective-permute-start(bf16[8,128,512]{2,1,0:T(8,128)(2,1)S(1)} %shard_map.64), channel_id=1, source_target_pairs={{0,1},{1,0},{2,3},{3,2},{4,5},{5,4},{6,7},{7,6},{8,9},{9,8},{10,11... | collective-permute-start | bytes 3145736 | tf_op jit(solution)/shard_map/ppermute | solution.py:17
  7.0 15.0 %all-to-all-start.1 = ((bf16[4,16,768]{2,1,0:T(8,128)(2,1)}), bf16[4,16,768]{2,1,0:T(8,128)(2,1)S(1)}, u32[]{:S(2)}, u32[]{:S(2)}) async-start(bf16[4,16,768]{2,1,0:T(8,128)(2,1)} %reshape.165), calls=%async_computation.1 | async-start | bytes 196608 | tf_op jit(solution)/shard_map/all_to_all | solution.py:102
  11.8 4.9 %copy-start.1 = (bf16[128,512]{1,0:T(8,128)(2,1)S(1)}, bf16[128,512]{1,0:T(8,128)(2,1)}, u32[]{:S(2)}) copy-start(bf16[128,512]{1,0:T(8,128)(2,1)} %rows_ref.3) | copy-start | bytes 393220
  15.7 1.0 copy-start.3
  16.7 19.5 %copy-start.6 = (s32[6144,1]{0,1:T(1,128)S(1)}, s32[6144,1]{0,1:T(1,128)}, u32[]{:S(2)}) copy-start(s32[6144,1]{0,1:T(1,128)} %param.11) | copy-start | bytes 73732
  21.9 38.2 %all-to-all-start = ((bf16[4,256,512]{2,1,0:T(8,128)(2,1)}), bf16[4,256,512]{2,1,0:T(8,128)(2,1)S(1)}, u32[]{:S(2)}, u32[]{:S(2)}) async-start(bf16[4,256,512]{2,1,0:T(8,128)(2,1)} %bitcast.2), calls=%async_computation | async-start | bytes 2097152 | tf_op jit(solution)/shard_map/all_to_all | solution.py:134
  33.4 39.2 %copy-start.4 = (bf16[128,512]{1,0:T(8,128)(2,1)S(1)}, bf16[128,512]{1,0:T(8,128)(2,1)}, u32[]{:S(2)}) copy-start(bf16[128,512]{1,0:T(8,128)(2,1)} %param.6) | copy-start | bytes 393220
  34.3 17.1 %collective-permute-start.2 = (bf16[8,16,768]{2,1,0:T(8,128)(2,1)S(1)}, bf16[8,16,768]{2,1,0:T(8,128)(2,1)S(1)}, u32[]{:S(2)}, u32[]{:S(2)}) collective-permute-start(bf16[8,16,768]{2,1,0:T(8,128)(2,1)S(1)} %constant_dynamic-update-slice_fusion), channel_id=1, source_target_pairs={{0,2},{2,0},{1,3},{3,1},{4,6},{6,4},{5,7},{7,5},{8,10},{10,8},{9,1... | collective-permute-start | bytes 589832 | tf_op jit(solution)/shard_map/ppermute | solution.py:17
  51.4 12.5 %collective-permute-start.3 = (bf16[8,32,768]{2,1,0:T(8,128)(2,1)S(1)}, bf16[8,32,768]{2,1,0:T(8,128)(2,1)S(1)}, u32[]{:S(2)}, u32[]{:S(2)}) collective-permute-start(bf16[8,32,768]{2,1,0:T(8,128)(2,1)S(1)} %pad_maximum_fusion.1), channel_id=1, source_target_pairs={{0,4},{4,8},{8,12},{12,0},{1,5},{5,9},{9,13},{13,1},{2,6},{6,10},{... | collective-permute-start | bytes 1179656 | tf_op jit(solution)/shard_map/ppermute | solution.py:26
  53.7 14.1 %collective-permute-start.4 = (bf16[8,32,768]{2,1,0:T(8,128)(2,1)S(1)}, bf16[8,32,768]{2,1,0:T(8,128)(2,1)S(1)}, u32[]{:S(2)}, u32[]{:S(2)}) collective-permute-start(bf16[8,32,768]{2,1,0:T(8,128)(2,1)S(1)} %pad_maximum_fusion.1), channel_id=1, source_target_pairs={{0,8},{4,12},{8,0},{12,4},{1,9},{5,13},{9,1},{13,5},{2,10},{6,14},... | collective-permute-start | bytes 1179656 | tf_op jit(solution)/shard_map/ppermute | solution.py:26
  58.2 13.7 %collective-permute-start.5 = (bf16[8,32,768]{2,1,0:T(8,128)(2,1)S(1)}, bf16[8,32,768]{2,1,0:T(8,128)(2,1)S(1)}, u32[]{:S(2)}, u32[]{:S(2)}) collective-permute-start(bf16[8,32,768]{2,1,0:T(8,128)(2,1)S(1)} %pad_maximum_fusion.1), channel_id=1, source_target_pairs={{0,12},{4,0},{8,4},{12,8},{1,13},{5,1},{9,5},{13,9},{2,14},{6,2},{... | collective-permute-start | bytes 1179656 | tf_op jit(solution)/shard_map/ppermute | solution.py:26
  60.3 12.3 %collective-permute-start.1 = (bf16[128,512]{1,0:T(8,128)(2,1)S(1)}, bf16[128,512]{1,0:T(8,128)(2,1)S(1)}, u32[]{:S(2)}, u32[]{:S(2)}) collective-permute-start(bf16[128,512]{1,0:T(8,128)(2,1)S(1)} %fusion.25), channel_id=1, source_target_pairs={{0,2},{2,0},{1,3},{3,1},{4,6},{6,4},{5,7},{7,5},{8,10},{10,8},{9,1... | collective-permute-start | bytes 393224 | tf_op jit(solution)/shard_map/ppermute | solution.py:17
  73.7 16.8 %collective-permute-start.6 = (bf16[8,128,768]{2,1,0:T(8,128)(2,1)S(1)}, bf16[8,128,768]{2,1,0:T(8,128)(2,1)S(1)}, u32[]{:S(2)}, u32[]{:S(2)}) collective-permute-start(bf16[8,128,768]{2,1,0:T(8,128)(2,1)S(1)} %pad_maximum_fusion), channel_id=1, source_target_pairs={{0,1},{1,0},{2,3},{3,2},{4,5},{5,4},{6,7},{7,6},{8,9},{9,8},{10,11... | collective-permute-start | bytes 4718600 | tf_op jit(solution)/shard_map/ppermute | solution.py:17
  76.2 35.9 %all-to-all-start.2 = ((bf16[48,8,512]{2,1,0:T(8,128)(2,1)}), bf16[48,8,512]{2,1,0:T(8,128)(2,1)S(1)}, u32[]{:S(2)}, u32[]{:S(2)}) async-start(bf16[48,8,512]{2,1,0:T(8,128)(2,1)} %bitcast.27), calls=%async_computation.2 | async-start | bytes 786432 | tf_op jit(solution)/shard_map/all_to_all | solution.py:150
  90.6 2.5 %copy-start.2 = (bf16[4,12,64,512]{3,2,1,0:T(8,128)(2,1)S(1)}, bf16[4,12,64,512]{3,2,1,0:T(8,128)(2,1)}, u32[]{:S(2)}) copy-start(bf16[4,12,64,512]{3,2,1,0:T(8,128)(2,1)} %copy.11) | copy-start | bytes 9437188

commit v4 on v3

--- a/solution.py
+++ b/solution.py
@@ -128,19 +128,18 @@
     summed = half_product(attn_out, w_out, my_core, n_x * n_yh, taken)
     block = after(block, summed)
     block = jnp.concatenate([block] + [shift(block, "x", k) for k in range(1, n_x)], axis=1)
-    weight = proj.reshape(n_z, n_yl, ds // groups, width).transpose(1, 0, 2, 3)
-    weight = weight.reshape(n_yl, part, width)
     summed = summed.reshape(n_x, n_yh * rows, width)
     summed = lax.all_to_all(summed, "x", 0, 0, tiled=True)
     summed = jnp.sum(summed.astype(f32), axis=0).reshape(n_yh, rows, width)
     given = pick(summed, 1 - my_yh).astype(bf16)
     kept = resid.astype(f32) + pick(summed, my_yh)
     taken = meet(given, "yh", 1)
-    taken, block, weight = lax.optimization_barrier((taken, block, weight))
     hidden = (kept + taken.astype(f32)).astype(bf16)
 
     packed = jnp.dot(selector, hidden, preferred_element_type=f32).astype(bf16)
     block = joined(after(block, packed), "core", 1)
+    weight = after(proj, packed).reshape(n_z, n_yl, ds // groups, width).transpose(1, 0, 2, 3)
+    weight = weight.reshape(n_yl, part, width)
     parts = lax.optimization_barrier(
         [jnp.dot(closing, rows16, preferred_element_type=f32).astype(bf16) for rows16 in block]
     )

time: 172 us -> 168 us (0.977)
  waiting for transfers between devices: 42.8 us -> 40.6 us
  local copies, waits for them, and re-layouts: 8.16 us -> 6.34 us
    transpose x1 -> x0, local copies, waits for them, and re-layouts: 3.92 us -> none  [local(): weight = proj.reshape(n_z, n_yl, ds // groups, width).transpose(1, 0, 2, 3)]
    all_to_all x1, waiting for transfers between devices: 17.6 us -> 15.5 us  [local(): lax.all_to_all(packed.reshape(groups, PAD, width), DP, 0, 0, tiled=True)]
    unnamed x16, local copies, waits for them, and re-layouts: 2.94 us -> 4.69 us
  transfers between devices with their start and end apart: 10 -> 10, of which waited for: 6 -> 6; matrix products, arithmetic and copies ran while one was open for 7% -> 5% of each run, Pallas kernels for 3% -> 3%
where the time goes in v4:
time: 168 us; the launch traced here: 165 us
  blocking collectives  53.7 us (32%)
  starting transfers between devices  46.8 us (28%)
  waiting for transfers between devices  40.6 us (24%)
  Pallas kernels  8.31 us (5%)
  matrix products  7.02 us (4%)
  local copies, waits for them, and re-layouts  6.34 us (4%)
    all_to_all x1, blocking collectives, local(): lax.all_to_all(partial_grad.astype(bf16).reshape(n_z, ds // groups, width...  34.3 us
    all_gather x1, blocking collectives, local(): mismatch = lax.all_gather(mismatch, 'yl', axis=0, tiled=True)  19.4 us
    ppermute x4, waiting for transfers between devices, meet(): lax.ppermute(value, axis, [(i, i ^ bit) for i in range(lax.axis_size(axis...  15.6 us
    all_to_all x1, waiting for transfers between devices, local(): lax.all_to_all(packed.reshape(groups, PAD, width), DP, 0, 0, tiled=True)  15.5 us
    all_to_all x1, starting transfers between devices, local(): lax.all_to_all(packed.reshape(groups, PAD, width), DP, 0, 0, tiled=True)  14.1 us
    all_to_all x1, starting transfers between devices, local(): summed = lax.all_to_all(summed, 'x', 0, 0, tiled=True)  11.5 us
    ppermute x3, waiting for transfers between devices, shift(): lax.ppermute(value, axis, [(i, (i + step) % size) for i in range(size)])  9.61 us
    ppermute x3, starting transfers between devices, shift(): lax.ppermute(value, axis, [(i, (i + step) % size) for i in range(size)])  8.66 us
  transfers between devices with their start and end apart: 10, of which 6 were waited for; matrix products, arithmetic and copies ran while one was open for 5% of the time, Pallas kernels for 3%

profile of v4, /device:TPU:6, one launch (start us, length us, event | category | flops | bytes accessed | tf_op | source)
XLA Modules:
  0.0 164.7 jit_solution(17109851674682862637)
XLA Ops:
  0.0 0.9 copy-done
  0.9 3.1 %shard_map.64 = bf16[8,128,512]{2,1,0:T(8,128)(2,1)S(1)} custom-call(s32[1]{0:T(128)} %bitcast.2.core_ref, bf16[128,512]{1,0:T(8,128)(2,1)S(1)} %copy-done, bf16[512,8192]{1,0:T(8,128)(2,1)} %weight_ref.3), custom_call_target="tpu_custom_call" | custom-call | flops 536870912 | bytes 5242880 | tf_op jit(solution)/shard_map/pallas_call | solution.py:59
  4.0 1.9 %collective-permute-start.1 = (bf16[8,128,512]{2,1,0:T(8,128)(2,1)S(1)}, bf16[8,128,512]{2,1,0:T(8,128)(2,1)S(1)}, u32[]{:S(2)}, u32[]{:S(2)}) collective-permute-start(bf16[8,128,512]{2,1,0:T(8,128)(2,1)S(1)} %shard_map.64), channel_id=1, source_target_pairs={{0,1},{1,0},{2,3},{3,2},{4,5},{5,4},{6,7},{7,6},{8,9},{9,8},{10,11... | collective-permute-start | bytes 3145736 | tf_op jit(solution)/shard_map/ppermute | solution.py:17
  5.9 0.2 reshape.166
  6.2 0.8 reshape.167
  7.0 4.9 %all-to-all-start = ((bf16[4,16,768]{2,1,0:T(8,128)(2,1)}), bf16[4,16,768]{2,1,0:T(8,128)(2,1)S(1)}, u32[]{:S(2)}, u32[]{:S(2)}) async-start(bf16[4,16,768]{2,1,0:T(8,128)(2,1)} %reshape.167), calls=%async_computation | async-start | bytes 196608 | tf_op jit(solution)/shard_map/all_to_all | solution.py:102
  11.9 1.0 copy-done.3
  12.8 5.3 %shard_map.65 = bf16[8,128,512]{2,1,0:T(8,128)(2,1)} custom-call(s32[1]{0:T(128)} %bitcast.1.core_ref, bf16[128,512]{1,0:T(8,128)(2,1)S(1)} %copy-done.1, bf16[512,8192]{1,0:T(8,128)(2,1)} %weight_ref.3, bf16[8,128,512]{2,1,0:T(8,128)(2,1)} %copy-done.3), custom_call_target="tpu_custom_call" | custom-call | flops 536870912 | bytes 5242880 | tf_op jit(solution)/shard_map/pallas_call | solution.py:59
  18.1 11.5 %all-to-all-start.1 = ((bf16[4,256,512]{2,1,0:T(8,128)(2,1)}), bf16[4,256,512]{2,1,0:T(8,128)(2,1)S(1)}, u32[]{:S(2)}, u32[]{:S(2)}) async-start(bf16[4,256,512]{2,1,0:T(8,128)(2,1)} %bitcast.7), calls=%async_computation.1 | async-start | bytes 2097152 | tf_op jit(solution)/shard_map/all_to_all | solution.py:132
  29.5 0.9 constant_dynamic-update-slice_fusion.1
  30.5 1.9 %collective-permute-start = (bf16[8,16,768]{2,1,0:T(8,128)(2,1)S(1)}, bf16[8,16,768]{2,1,0:T(8,128)(2,1)S(1)}, u32[]{:S(2)}, u32[]{:S(2)}) collective-permute-start(bf16[8,16,768]{2,1,0:T(8,128)(2,1)S(1)} %constant_dynamic-update-slice_fusion), channel_id=1, source_target_pairs={{0,2},{2,0},{1,3},{3,1},{4,6},{6,4},{5,7},{7,5},{8,10},{10,8},{9,1... | collective-permute-start | bytes 589832 | tf_op jit(solution)/shard_map/ppermute | solution.py:17
  32.5 0.2 convert_reduce_fusion.2
  32.6 14.9 %collective-permute-done = bf16[8,16,768]{2,1,0:T(8,128)(2,1)S(1)} collective-permute-done((bf16[8,16,768]{2,1,0:T(8,128)(2,1)S(1)}, bf16[8,16,768]{2,1,0:T(8,128)(2,1)S(1)}, u32[]{:S(2)}, u32[]{:S(2)}) %collective-permute-start) | collective-permute-done | bytes 196640 | tf_op jit(solution)/shard_map/ppermute | solution.py:17
  47.6 2.2 %collective-permute-start.2 = (bf16[8,32,768]{2,1,0:T(8,128)(2,1)S(1)}, bf16[8,32,768]{2,1,0:T(8,128)(2,1)S(1)}, u32[]{:S(2)}, u32[]{:S(2)}) collective-permute-start(bf16[8,32,768]{2,1,0:T(8,128)(2,1)S(1)} %pad_maximum_fusion.1), channel_id=1, source_target_pairs={{0,4},{4,8},{8,12},{12,0},{1,5},{5,9},{9,13},{13,1},{2,6},{6,10},{... | collective-permute-start | bytes 1179656 | tf_op jit(solution)/shard_map/ppermute | solution.py:26
  49.8 4.5 %collective-permute-start.3 = (bf16[8,32,768]{2,1,0:T(8,128)(2,1)S(1)}, bf16[8,32,768]{2,1,0:T(8,128)(2,1)S(1)}, u32[]{:S(2)}, u32[]{:S(2)}) collective-permute-start(bf16[8,32,768]{2,1,0:T(8,128)(2,1)S(1)} %pad_maximum_fusion.1), channel_id=1, source_target_pairs={{0,8},{4,12},{8,0},{12,4},{1,9},{5,13},{9,1},{13,5},{2,10},{6,14},... | collective-permute-start | bytes 1179656 | tf_op jit(solution)/shard_map/ppermute | solution.py:26
  54.3 1.9 %collective-permute-start.4 = (bf16[8,32,768]{2,1,0:T(8,128)(2,1)S(1)}, bf16[8,32,768]{2,1,0:T(8,128)(2,1)S(1)}, u32[]{:S(2)}, u32[]{:S(2)}) collective-permute-start(bf16[8,32,768]{2,1,0:T(8,128)(2,1)S(1)} %pad_maximum_fusion.1), channel_id=1, source_target_pairs={{0,12},{4,0},{8,4},{12,8},{1,13},{5,1},{9,5},{13,9},{2,14},{6,2},{... | collective-permute-start | bytes 1179656 | tf_op jit(solution)/shard_map/ppermute | solution.py:26
  56.5 1.9 %collective-permute-start.5 = (bf16[128,512]{1,0:T(8,128)(2,1)S(1)}, bf16[128,512]{1,0:T(8,128)(2,1)S(1)}, u32[]{:S(2)}, u32[]{:S(2)}) collective-permute-start(bf16[128,512]{1,0:T(8,128)(2,1)S(1)} %fusion.16), channel_id=1, source_target_pairs={{0,2},{2,0},{1,3},{3,1},{4,6},{6,4},{5,7},{7,5},{8,10},{10,8},{9,1... | collective-permute-start | bytes 393224 | tf_op jit(solution)/shard_map/ppermute | solution.py:17
  58.4 1.6 collective-permute-done.2
  60.1 3.9 %collective-permute-done.3 = bf16[8,32,768]{2,1,0:T(8,128)(2,1)S(1)} collective-permute-done((bf16[8,32,768]{2,1,0:T(8,128)(2,1)S(1)}, bf16[8,32,768]{2,1,0:T(8,128)(2,1)S(1)}, u32[]{:S(2)}, u32[]{:S(2)}) %collective-permute-start.3) | collective-permute-done | bytes 393248 | tf_op jit(solution)/shard_map/ppermute | solution.py:26
  63.9 4.1 %collective-permute-done.4 = bf16[8,32,768]{2,1,0:T(8,128)(2,1)S(1)} collective-permute-done((bf16[8,32,768]{2,1,0:T(8,128)(2,1)S(1)}, bf16[8,32,768]{2,1,0:T(8,128)(2,1)S(1)}, u32[]{:S(2)}, u32[]{:S(2)}) %collective-permute-start.4) | collective-permute-done | bytes 393248 | tf_op jit(solution)/shard_map/ppermute | solution.py:26
  68.1 0.6 collective-permute-done.5
  68.8 1.0 convolution_convert_fusion
  69.8 1.9 %collective-permute-start.6 = (bf16[8,128,768]{2,1,0:T(8,128)(2,1)S(1)}, bf16[8,128,768]{2,1,0:T(8,128)(2,1)S(1)}, u32[]{:S(2)}, u32[]{:S(2)}) collective-permute-start(bf16[8,128,768]{2,1,0:T(8,128)(2,1)S(1)} %pad_maximum_fusion), channel_id=1, source_target_pairs={{0,1},{1,0},{2,3},{3,2},{4,5},{5,4},{6,7},{7,6},{8,9},{9,8},{10,11... | collective-permute-start | bytes 4718600 | tf_op jit(solution)/shard_map/ppermute | solution.py:17
  72.1 0.2 fusion.4
  72.3 14.1 %all-to-all-start.2 = ((bf16[48,8,512]{2,1,0:T(8,128)(2,1)}), bf16[48,8,512]{2,1,0:T(8,128)(2,1)S(1)}, u32[]{:S(2)}, u32[]{:S(2)}) async-start(bf16[48,8,512]{2,1,0:T(8,128)(2,1)} %bitcast.27), calls=%async_computation.2 | async-start | bytes 786432 | tf_op jit(solution)/shard_map/all_to_all | solution.py:149
  86.6 1.8 %copy-done.2 = bf16[3072,512]{1,0:T(8,128)(2,1)S(1)} copy-done((bf16[3072,512]{1,0:T(8,128)(2,1)S(1)}, bf16[3072,512]{1,0:T(8,128)(2,1)}, u32[]{:S(2)}) %copy-start.2) | copy-done | bytes 3145752
  88.4 0.3 fusion.40
  88.8 0.3 convolution_convert_fusion.1
  89.1 0.3 convolution_convert_fusion.2
  89.5 0.3 convolution_convert_fusion.3
  89.8 0.3 convolution_convert_fusion.4
  90.1 0.3 convolution_convert_fusion.5
  90.4 0.3 convolution_convert_fusion.6
  90.7 0.3 convolution_convert_fusion.7
  91.0 0.3 convolution_convert_fusion.8
  91.3 0.3 fusion.41
  91.7 0.4 convolution_add_fusion.2
  92.0 0.4 convolution_add_fusion.1
  92.4 0.4 convolution_add_fusion
  92.8 15.5 %all-to-all-done.2 = bf16[48,8,512]{2,1,0:T(8,128)(2,1)S(1)} async-done(((bf16[48,8,512]{2,1,0:T(8,128)(2,1)}), bf16[48,8,512]{2,1,0:T(8,128)(2,1)S(1)}, u32[]{:S(2)}, u32[]{:S(2)}) %all-to-all-start.2) | async-done | bytes 393248 | tf_op jit(solution)/shard_map/all_to_all | solution.py:149
  108.2 0.3 fusion.2
  108.5 19.4 %all_gather.3 = bf16[960,512]{1,0:T(8,128)(2,1)S(1)} all-gather(bf16[240,512]{1,0:T(8,128)(2,1)S(1)} %fusion.2), channel_id=1, replica_groups=mesh['z'=12,'yl'=4,'x'=4,'yh'=2,'core'=2] {'yl'}, dimensions={0}, use_global_device_ids=true | all-gather | bytes 1228800 | tf_op jit(solution)/shard_map/all_gather | solution.py:155
  128.0 0.4 fusion.10
  128.4 0.4 fusion.12
  128.8 0.4 fusion.8
  129.2 0.4 add_convert_fusion
  129.6 34.3 %all_to_all.20 = bf16[12,64,512]{2,1,0:T(8,128)(2,1)S(1)} all-to-all(bf16[12,64,512]{2,1,0:T(8,128)(2,1)S(1)} %bitcast.79), channel_id=1, replica_groups=mesh['z'=12,'yl'=4,'x'=4,'yh'=2,'core'=2] {'z'}, dimensions={0} | all-to-all | bytes 1572864 | tf_op jit(solution)/shard_map/all_to_all | solution.py:163
  163.9 0.8 convert_reduce_fusion.1
  (32 shorter events, 1.0 us)
Async XLA Ops:
  0.0 0.9 copy-start
  0.9 5.0 %copy-start.5 = (bf16[15,3072]{1,0:T(8,128)(2,1)S(1)}, bf16[15,3072]{1,0:T(8,128)(2,1)}, u32[]{:S(2)}) copy-start(bf16[15,3072]{1,0:T(8,128)(2,1)} %param.10) | copy-start | bytes 276484
  0.9 11.9 %copy-start.1 = (bf16[128,512]{1,0:T(8,128)(2,1)S(1)}, bf16[128,512]{1,0:T(8,128)(2,1)}, u32[]{:S(2)}) copy-start(bf16[128,512]{1,0:T(8,128)(2,1)} %rows_ref.3) | copy-start | bytes 393220
  4.0 7.9 %collective-permute-start.1 = (bf16[8,128,512]{2,1,0:T(8,128)(2,1)S(1)}, bf16[8,128,512]{2,1,0:T(8,128)(2,1)S(1)}, u32[]{:S(2)}, u32[]{:S(2)}) collective-permute-start(bf16[8,128,512]{2,1,0:T(8,128)(2,1)S(1)} %shard_map.64), channel_id=1, source_target_pairs={{0,1},{1,0},{2,3},{3,2},{4,5},{5,4},{6,7},{7,6},{8,9},{9,8},{10,11... | collective-permute-start | bytes 3145736 | tf_op jit(solution)/shard_map/ppermute | solution.py:17
  7.0 11.1 %all-to-all-start = ((bf16[4,16,768]{2,1,0:T(8,128)(2,1)}), bf16[4,16,768]{2,1,0:T(8,128)(2,1)S(1)}, u32[]{:S(2)}, u32[]{:S(2)}) async-start(bf16[4,16,768]{2,1,0:T(8,128)(2,1)} %reshape.167), calls=%async_computation | async-start | bytes 196608 | tf_op jit(solution)/shard_map/all_to_all | solution.py:102
  11.9 1.0 copy-start.3
  12.8 19.6 %copy-start.6 = (s32[6144,1]{0,1:T(1,128)S(1)}, s32[6144,1]{0,1:T(1,128)}, u32[]{:S(2)}) copy-start(s32[6144,1]{0,1:T(1,128)} %param.11) | copy-start | bytes 73732
  18.1 38.2 %all-to-all-start.1 = ((bf16[4,256,512]{2,1,0:T(8,128)(2,1)}), bf16[4,256,512]{2,1,0:T(8,128)(2,1)S(1)}, u32[]{:S(2)}, u32[]{:S(2)}) async-start(bf16[4,256,512]{2,1,0:T(8,128)(2,1)} %bitcast.7), calls=%async_computation.1 | async-start | bytes 2097152 | tf_op jit(solution)/shard_map/all_to_all | solution.py:132
  29.5 39.2 %copy-start.4 = (bf16[128,512]{1,0:T(8,128)(2,1)S(1)}, bf16[128,512]{1,0:T(8,128)(2,1)}, u32[]{:S(2)}) copy-start(bf16[128,512]{1,0:T(8,128)(2,1)} %param.6) | copy-start | bytes 393220
  30.5 17.1 %collective-permute-start = (bf16[8,16,768]{2,1,0:T(8,128)(2,1)S(1)}, bf16[8,16,768]{2,1,0:T(8,128)(2,1)S(1)}, u32[]{:S(2)}, u32[]{:S(2)}) collective-permute-start(bf16[8,16,768]{2,1,0:T(8,128)(2,1)S(1)} %constant_dynamic-update-slice_fusion), channel_id=1, source_target_pairs={{0,2},{2,0},{1,3},{3,1},{4,6},{6,4},{5,7},{7,5},{8,10},{10,8},{9,1... | collective-permute-start | bytes 589832 | tf_op jit(solution)/shard_map/ppermute | solution.py:17
  47.6 12.5 %collective-permute-start.2 = (bf16[8,32,768]{2,1,0:T(8,128)(2,1)S(1)}, bf16[8,32,768]{2,1,0:T(8,128)(2,1)S(1)}, u32[]{:S(2)}, u32[]{:S(2)}) collective-permute-start(bf16[8,32,768]{2,1,0:T(8,128)(2,1)S(1)} %pad_maximum_fusion.1), channel_id=1, source_target_pairs={{0,4},{4,8},{8,12},{12,0},{1,5},{5,9},{9,13},{13,1},{2,6},{6,10},{... | collective-permute-start | bytes 1179656 | tf_op jit(solution)/shard_map/ppermute | solution.py:26
  49.8 14.1 %collective-permute-start.3 = (bf16[8,32,768]{2,1,0:T(8,128)(2,1)S(1)}, bf16[8,32,768]{2,1,0:T(8,128)(2,1)S(1)}, u32[]{:S(2)}, u32[]{:S(2)}) collective-permute-start(bf16[8,32,768]{2,1,0:T(8,128)(2,1)S(1)} %pad_maximum_fusion.1), channel_id=1, source_target_pairs={{0,8},{4,12},{8,0},{12,4},{1,9},{5,13},{9,1},{13,5},{2,10},{6,14},... | collective-permute-start | bytes 1179656 | tf_op jit(solution)/shard_map/ppermute | solution.py:26
  54.3 13.7 %collective-permute-start.4 = (bf16[8,32,768]{2,1,0:T(8,128)(2,1)S(1)}, bf16[8,32,768]{2,1,0:T(8,128)(2,1)S(1)}, u32[]{:S(2)}, u32[]{:S(2)}) collective-permute-start(bf16[8,32,768]{2,1,0:T(8,128)(2,1)S(1)} %pad_maximum_fusion.1), channel_id=1, source_target_pairs={{0,12},{4,0},{8,4},{12,8},{1,13},{5,1},{9,5},{13,9},{2,14},{6,2},{... | collective-permute-start | bytes 1179656 | tf_op jit(solution)/shard_map/ppermute | solution.py:26
  56.5 12.3 %collective-permute-start.5 = (bf16[128,512]{1,0:T(8,128)(2,1)S(1)}, bf16[128,512]{1,0:T(8,128)(2,1)S(1)}, u32[]{:S(2)}, u32[]{:S(2)}) collective-permute-start(bf16[128,512]{1,0:T(8,128)(2,1)S(1)} %fusion.16), channel_id=1, source_target_pairs={{0,2},{2,0},{1,3},{3,1},{4,6},{6,4},{5,7},{7,5},{8,10},{10,8},{9,1... | collective-permute-start | bytes 393224 | tf_op jit(solution)/shard_map/ppermute | solution.py:17
  69.8 18.9 %collective-permute-start.6 = (bf16[8,128,768]{2,1,0:T(8,128)(2,1)S(1)}, bf16[8,128,768]{2,1,0:T(8,128)(2,1)S(1)}, u32[]{:S(2)}, u32[]{:S(2)}) collective-permute-start(bf16[8,128,768]{2,1,0:T(8,128)(2,1)S(1)} %pad_maximum_fusion), channel_id=1, source_target_pairs={{0,1},{1,0},{2,3},{3,2},{4,5},{5,4},{6,7},{7,6},{8,9},{9,8},{10,11... | collective-permute-start | bytes 4718600 | tf_op jit(solution)/shard_map/ppermute | solution.py:17
  72.3 35.9 %all-to-all-start.2 = ((bf16[48,8,512]{2,1,0:T(8,128)(2,1)}), bf16[48,8,512]{2,1,0:T(8,128)(2,1)S(1)}, u32[]{:S(2)}, u32[]{:S(2)}) async-start(bf16[48,8,512]{2,1,0:T(8,128)(2,1)} %bitcast.27), calls=%async_computation.2 | async-start | bytes 786432 | tf_op jit(solution)/shard_map/all_to_all | solution.py:149
  86.5 1.9 %copy-start.2 = (bf16[3072,512]{1,0:T(8,128)(2,1)S(1)}, bf16[3072,512]{1,0:T(8,128)(2,1)}, u32[]{:S(2)}) copy-start(bf16[3072,512]{1,0:T(8,128)(2,1)} %param.9) | copy-start | bytes 9437188

commit v5 on v4

--- a/solution.py
+++ b/solution.py
@@ -35,21 +35,27 @@
 
 
 def product_kernel(core_ref, rows_ref, weight_ref, *refs):
-    *added, out_ref, held, arrived = refs
+    *added, out_ref, rows_held, held, added_held, rows_sem, sems, added_sems = refs
     blocks, _, width = held.shape
+    rows_copy = pltpu.make_async_copy(rows_ref, rows_held, rows_sem)
     copies = []
     for k in range(blocks):
         first = pl.multiple_of((2 * k + core_ref[0]) * width, width)
-        copies.append(
-            pltpu.make_async_copy(weight_ref.at[:, pl.ds(first, width)], held.at[k], arrived.at[k])
-        )
-    for copy in copies:
-        copy.start()
-    for k, copy in enumerate(copies):
-        copy.wait()
-        block = jnp.dot(rows_ref[...], held[k], preferred_element_type=f32)
+        pair = [pltpu.make_async_copy(weight_ref.at[:, pl.ds(first, width)], held.at[k], sems.at[k])]
         for ref in added:
-            block = block + ref[k].astype(f32)
+            pair.append(pltpu.make_async_copy(ref.at[k], added_held.at[k], added_sems.at[k]))
+        copies.append(pair)
+    rows_copy.start()
+    for pair in copies:
+        for copy in pair:
+            copy.start()
+    rows_copy.wait()
+    for k, pair in enumerate(copies):
+        for copy in pair:
+            copy.wait()
+        block = jnp.dot(rows_held[...], held[k], preferred_element_type=f32)
+        if added:
+            block = block + added_held[k].astype(f32)
         out_ref[k] = block.astype(bf16)
 
 
@@ -60,14 +66,18 @@
         product_kernel,
         in_specs=[
             pl.BlockSpec(memory_space=pltpu.SMEM),
-            pl.BlockSpec(memory_space=pltpu.VMEM),
+            pl.BlockSpec(memory_space=pltpu.HBM),
             pl.BlockSpec(memory_space=pltpu.HBM),
         ]
-        + [pl.BlockSpec(memory_space=pltpu.VMEM) for _ in added],
+        + [pl.BlockSpec(memory_space=pltpu.HBM) for _ in added],
         out_specs=pl.BlockSpec(memory_space=pltpu.VMEM),
         out_shape=jax.ShapeDtypeStruct((blocks, n, width), bf16),
         scratch_shapes=[
+            pltpu.VMEM((n, depth), bf16),
             pltpu.VMEM((blocks, depth, width), bf16),
+            pltpu.VMEM((blocks, n, width), bf16),
+            pltpu.SemaphoreType.DMA,
+            pltpu.SemaphoreType.DMA((blocks,)),
             pltpu.SemaphoreType.DMA((blocks,)),
         ],
         cost_estimate=pl.CostEstimate(
@@ -126,14 +136,14 @@
     ).astype(bf16)
 
     summed = half_product(attn_out, w_out, my_core, n_x * n_yh, taken)
-    block = after(block, summed)
-    block = jnp.concatenate([block] + [shift(block, "x", k) for k in range(1, n_x)], axis=1)
     summed = summed.reshape(n_x, n_yh * rows, width)
     summed = lax.all_to_all(summed, "x", 0, 0, tiled=True)
     summed = jnp.sum(summed.astype(f32), axis=0).reshape(n_yh, rows, width)
     given = pick(summed, 1 - my_yh).astype(bf16)
     kept = resid.astype(f32) + pick(summed, my_yh)
     taken = meet(given, "yh", 1)
+    block = after(block, given)
+    block = jnp.concatenate([block] + [shift(block, "x", k) for k in range(1, n_x)], axis=1)
     hidden = (kept + taken.astype(f32)).astype(bf16)
 
     packed = jnp.dot(selector, hidden, preferred_element_type=f32).astype(bf16)

time: 168 us -> 166 us (0.988)
    ppermute x3, waiting for transfers between devices: 9.61 us -> 0.01 us  [shift(): lax.ppermute(value, axis, [(i, (i + step) % size) for i in range(size)])]
    ppermute x4, waiting for transfers between devices: 15.6 us -> 24.7 us  [meet(): lax.ppermute(value, axis, [(i, i ^ bit) for i in range(lax.axis_size(axis...]
    unnamed x16 -> x14, local copies, waits for them, and re-layouts: 4.69 us -> 2.89 us
    slice x1, local copies, waits for them, and re-layouts: 0.34 us -> 2.06 us  [local(): weight[k]]
  transfers between devices with their start and end apart: 10 -> 10, of which waited for: 6 -> 4; matrix products, arithmetic and copies ran while one was open for 5% -> 6% of each run, Pallas kernels for 3% -> 3%
where the time goes in v5:
time: 166 us; the launch traced here: 163 us
  blocking collectives  53.7 us (32%)
  starting transfers between devices  45.8 us (28%)
  waiting for transfers between devices  41 us (25%)
  Pallas kernels  7.53 us (5%)
  matrix products  7.02 us (4%)
  local copies, waits for them, and re-layouts  6.26 us (4%)
    all_to_all x1, blocking collectives, local(): lax.all_to_all(partial_grad.astype(bf16).reshape(n_z, ds // groups, width...  34.3 us
    ppermute x4, waiting for transfers between devices, meet(): lax.ppermute(value, axis, [(i, i ^ bit) for i in range(lax.axis_size(axis...  24.7 us
    all_gather x1, blocking collectives, local(): mismatch = lax.all_gather(mismatch, 'yl', axis=0, tiled=True)  19.4 us
    all_to_all x1, waiting for transfers between devices, local(): lax.all_to_all(packed.reshape(groups, PAD, width), DP, 0, 0, tiled=True)  15.5 us
    all_to_all x1, starting transfers between devices, local(): lax.all_to_all(packed.reshape(groups, PAD, width), DP, 0, 0, tiled=True)  13.2 us
    all_to_all x1, starting transfers between devices, local(): summed = lax.all_to_all(summed, 'x', 0, 0, tiled=True)  11.4 us
    ppermute x3, starting transfers between devices, shift(): lax.ppermute(value, axis, [(i, (i + step) % size) for i in range(size)])  8.66 us
    ppermute x4, starting transfers between devices, meet(): lax.ppermute(value, axis, [(i, i ^ bit) for i in range(lax.axis_size(axis...  7.68 us
  transfers between devices with their start and end apart: 10, of which 4 were waited for; matrix products, arithmetic and copies ran while one was open for 6% of the time, Pallas kernels for 3%

profile of v5, /device:TPU:6, one launch (start us, length us, event | category | flops | bytes accessed | tf_op | source)
XLA Modules:
  0.0 163.2 jit_solution(17205568925349208243)
XLA Ops:
  0.0 0.9 copy-done
  0.9 3.2 %shard_map.64 = bf16[8,128,512]{2,1,0:T(8,128)(2,1)S(1)} custom-call(s32[1]{0:T(128)} %bitcast.2.core_ref, bf16[128,512]{1,0:T(8,128)(2,1)S(1)} %copy-done, bf16[512,8192]{1,0:T(8,128)(2,1)} %weight_ref.3), custom_call_target="tpu_custom_call" | custom-call | flops 536870912 | bytes 5242880 | tf_op jit(solution)/shard_map/pallas_call | solution.py:65
  4.1 1.9 %collective-permute-start.1 = (bf16[8,128,512]{2,1,0:T(8,128)(2,1)S(1)}, bf16[8,128,512]{2,1,0:T(8,128)(2,1)S(1)}, u32[]{:S(2)}, u32[]{:S(2)}) collective-permute-start(bf16[8,128,512]{2,1,0:T(8,128)(2,1)S(1)} %shard_map.64), channel_id=1, source_target_pairs={{0,1},{1,0},{2,3},{3,2},{4,5},{5,4},{6,7},{7,6},{8,9},{9,8},{10,11... | collective-permute-start | bytes 3145736 | tf_op jit(solution)/shard_map/ppermute | solution.py:17
  6.1 0.2 reshape.166
  6.3 0.8 reshape.167
  7.1 4.9 %all-to-all-start = ((bf16[4,16,768]{2,1,0:T(8,128)(2,1)}), bf16[4,16,768]{2,1,0:T(8,128)(2,1)S(1)}, u32[]{:S(2)}, u32[]{:S(2)}) async-start(bf16[4,16,768]{2,1,0:T(8,128)(2,1)} %reshape.167), calls=%async_computation | async-start | bytes 196608 | tf_op jit(solution)/shard_map/all_to_all | solution.py:112
  12.0 1.0 copy-done.2
  13.0 4.3 %shard_map.65 = bf16[8,128,512]{2,1,0:T(8,128)(2,1)} custom-call(s32[1]{0:T(128)} %bitcast.1.core_ref, bf16[128,512]{1,0:T(8,128)(2,1)S(1)} %copy-done.1, bf16[512,8192]{1,0:T(8,128)(2,1)} %weight_ref.3, bf16[8,128,512]{2,1,0:T(8,128)(2,1)} %copy-done.2), custom_call_target="tpu_custom_call" | custom-call | flops 536870912 | bytes 5242880 | tf_op jit(solution)/shard_map/pallas_call | solution.py:65
  17.3 0.7 all-to-all-done
  18.0 11.4 %all-to-all-start.1 = ((bf16[4,256,512]{2,1,0:T(8,128)(2,1)}), bf16[4,256,512]{2,1,0:T(8,128)(2,1)S(1)}, u32[]{:S(2)}, u32[]{:S(2)}) async-start(bf16[4,256,512]{2,1,0:T(8,128)(2,1)} %bitcast.3), calls=%async_computation.1 | async-start | bytes 2097152 | tf_op jit(solution)/shard_map/all_to_all | solution.py:140
  29.4 0.9 constant_dynamic-update-slice_fusion.1
  30.3 1.9 %collective-permute-start = (bf16[8,16,768]{2,1,0:T(8,128)(2,1)S(1)}, bf16[8,16,768]{2,1,0:T(8,128)(2,1)S(1)}, u32[]{:S(2)}, u32[]{:S(2)}) collective-permute-start(bf16[8,16,768]{2,1,0:T(8,128)(2,1)S(1)} %constant_dynamic-update-slice_fusion), channel_id=1, source_target_pairs={{0,2},{2,0},{1,3},{3,1},{4,6},{6,4},{5,7},{7,5},{8,10},{10,8},{9,1... | collective-permute-start | bytes 589832 | tf_op jit(solution)/shard_map/ppermute | solution.py:17
  32.3 0.2 convert_reduce_fusion.2
  32.5 14.4 %collective-permute-done = bf16[8,16,768]{2,1,0:T(8,128)(2,1)S(1)} collective-permute-done((bf16[8,16,768]{2,1,0:T(8,128)(2,1)S(1)}, bf16[8,16,768]{2,1,0:T(8,128)(2,1)S(1)}, u32[]{:S(2)}, u32[]{:S(2)}) %collective-permute-start) | collective-permute-done | bytes 196640 | tf_op jit(solution)/shard_map/ppermute | solution.py:17
  46.9 0.1 convert_reduce_fusion
  47.1 2.2 %collective-permute-start.2 = (bf16[8,32,768]{2,1,0:T(8,128)(2,1)S(1)}, bf16[8,32,768]{2,1,0:T(8,128)(2,1)S(1)}, u32[]{:S(2)}, u32[]{:S(2)}) collective-permute-start(bf16[8,32,768]{2,1,0:T(8,128)(2,1)S(1)} %pad_maximum_fusion.1), channel_id=1, source_target_pairs={{0,4},{4,8},{8,12},{12,0},{1,5},{5,9},{9,13},{13,1},{2,6},{6,10},{... | collective-permute-start | bytes 1179656 | tf_op jit(solution)/shard_map/ppermute | solution.py:26
  49.3 4.5 %collective-permute-start.3 = (bf16[8,32,768]{2,1,0:T(8,128)(2,1)S(1)}, bf16[8,32,768]{2,1,0:T(8,128)(2,1)S(1)}, u32[]{:S(2)}, u32[]{:S(2)}) collective-permute-start(bf16[8,32,768]{2,1,0:T(8,128)(2,1)S(1)} %pad_maximum_fusion.1), channel_id=1, source_target_pairs={{0,8},{4,12},{8,0},{12,4},{1,9},{5,13},{9,1},{13,5},{2,10},{6,14},... | collective-permute-start | bytes 1179656 | tf_op jit(solution)/shard_map/ppermute | solution.py:26
  53.9 1.9 %collective-permute-start.4 = (bf16[8,32,768]{2,1,0:T(8,128)(2,1)S(1)}, bf16[8,32,768]{2,1,0:T(8,128)(2,1)S(1)}, u32[]{:S(2)}, u32[]{:S(2)}) collective-permute-start(bf16[8,32,768]{2,1,0:T(8,128)(2,1)S(1)} %pad_maximum_fusion.1), channel_id=1, source_target_pairs={{0,12},{4,0},{8,4},{12,8},{1,13},{5,1},{9,5},{13,9},{2,14},{6,2},{... | collective-permute-start | bytes 1179656 | tf_op jit(solution)/shard_map/ppermute | solution.py:26
  55.8 1.9 %collective-permute-start.5 = (bf16[128,512]{1,0:T(8,128)(2,1)S(1)}, bf16[128,512]{1,0:T(8,128)(2,1)S(1)}, u32[]{:S(2)}, u32[]{:S(2)}) collective-permute-start(bf16[128,512]{1,0:T(8,128)(2,1)S(1)} %fusion.16), channel_id=1, source_target_pairs={{0,2},{2,0},{1,3},{3,1},{4,6},{6,4},{5,7},{7,5},{8,10},{10,8},{9,1... | collective-permute-start | bytes 393224 | tf_op jit(solution)/shard_map/ppermute | solution.py:17
  57.7 10.3 %collective-permute-done.5 = bf16[128,512]{1,0:T(8,128)(2,1)S(1)} collective-permute-done((bf16[128,512]{1,0:T(8,128)(2,1)S(1)}, bf16[128,512]{1,0:T(8,128)(2,1)S(1)}, u32[]{:S(2)}, u32[]{:S(2)}) %collective-permute-start.5) | collective-permute-done | bytes 131104 | tf_op jit(solution)/shard_map/ppermute | solution.py:17
  68.1 1.0 convolution_convert_fusion
  69.2 1.9 %collective-permute-start.6 = (bf16[8,128,768]{2,1,0:T(8,128)(2,1)S(1)}, bf16[8,128,768]{2,1,0:T(8,128)(2,1)S(1)}, u32[]{:S(2)}, u32[]{:S(2)}) collective-permute-start(bf16[8,128,768]{2,1,0:T(8,128)(2,1)S(1)} %pad_maximum_fusion), channel_id=1, source_target_pairs={{0,1},{1,0},{2,3},{3,2},{4,5},{5,4},{6,7},{7,6},{8,9},{9,8},{10,11... | collective-permute-start | bytes 4718600 | tf_op jit(solution)/shard_map/ppermute | solution.py:17
  71.2 0.1 convert_reduce_fusion.3
  71.3 0.1 reshape.176
  71.5 0.2 fusion.4
  71.8 13.2 %all-to-all-start.2 = ((bf16[48,8,512]{2,1,0:T(8,128)(2,1)}), bf16[48,8,512]{2,1,0:T(8,128)(2,1)S(1)}, u32[]{:S(2)}, u32[]{:S(2)}) async-start(bf16[48,8,512]{2,1,0:T(8,128)(2,1)} %bitcast.27), calls=%async_computation.2 | async-start | bytes 786432 | tf_op jit(solution)/shard_map/all_to_all | solution.py:159
  85.0 2.1 %fusion.40 = (bf16[1,12,64,512]{3,2,0,1:T(8,128)(2,1)S(1)}, bf16[1,12,64,512]{3,2,0,1:T(8,128)(2,1)S(1)}, bf16[1,12,64,512]{3,2,0,1:T(8,128)(2,1)S(1)}, bf16[1,12,64,512]{3,2,0,1:T(8,128)(2,1)S(1)}) fusion(bf16[4,12,64,512]{3,2,0,1:T(8,128)(2,1)} %bitcast.80), kind=kLoop, calls=%fused_computation.104 | loop fusion | bytes 6291456 | tf_op jit(solution)/shard_map/slice | solution.py:157
  87.3 0.3 convolution_convert_fusion.1
  87.6 0.3 convolution_convert_fusion.2
  87.9 0.3 convolution_convert_fusion.3
  88.2 0.3 convolution_convert_fusion.4
  88.5 0.3 convolution_convert_fusion.5
  88.8 0.3 convolution_convert_fusion.6
  89.1 0.3 convolution_convert_fusion.7
  89.4 0.3 convolution_convert_fusion.8
  89.7 0.3 fusion.41
  90.1 0.4 convolution_add_fusion.2
  90.4 0.4 convolution_add_fusion.1
  90.8 0.4 convolution_add_fusion
  91.2 15.5 %all-to-all-done.2 = bf16[48,8,512]{2,1,0:T(8,128)(2,1)S(1)} async-done(((bf16[48,8,512]{2,1,0:T(8,128)(2,1)}), bf16[48,8,512]{2,1,0:T(8,128)(2,1)S(1)}, u32[]{:S(2)}, u32[]{:S(2)}) %all-to-all-start.2) | async-done | bytes 393248 | tf_op jit(solution)/shard_map/all_to_all | solution.py:159
  106.7 0.3 fusion.2
  107.0 19.4 %all_gather.3 = bf16[960,512]{1,0:T(8,128)(2,1)S(1)} all-gather(bf16[240,512]{1,0:T(8,128)(2,1)S(1)} %fusion.2), channel_id=1, replica_groups=mesh['z'=12,'yl'=4,'x'=4,'yh'=2,'core'=2] {'yl'}, dimensions={0}, use_global_device_ids=true | all-gather | bytes 1228800 | tf_op jit(solution)/shard_map/all_gather | solution.py:165
  126.5 0.4 fusion.10
  126.9 0.4 fusion.12
  127.3 0.4 fusion.8
  127.7 0.4 add_convert_fusion
  128.1 34.3 %all_to_all.20 = bf16[12,64,512]{2,1,0:T(8,128)(2,1)S(1)} all-to-all(bf16[12,64,512]{2,1,0:T(8,128)(2,1)S(1)} %bitcast.79), channel_id=1, replica_groups=mesh['z'=12,'yl'=4,'x'=4,'yh'=2,'core'=2] {'z'}, dimensions={0} | all-to-all | bytes 1572864 | tf_op jit(solution)/shard_map/all_to_all | solution.py:173
  162.4 0.8 convert_reduce_fusion.1
  (30 shorter events, 0.6 us)
Async XLA Ops:
  0.0 0.9 copy-start
  0.9 5.2 %copy-start.4 = (bf16[15,3072]{1,0:T(8,128)(2,1)S(1)}, bf16[15,3072]{1,0:T(8,128)(2,1)}, u32[]{:S(2)}) copy-start(bf16[15,3072]{1,0:T(8,128)(2,1)} %param.10) | copy-start | bytes 276484
  0.9 12.1 %copy-start.1 = (bf16[128,512]{1,0:T(8,128)(2,1)S(1)}, bf16[128,512]{1,0:T(8,128)(2,1)}, u32[]{:S(2)}) copy-start(bf16[128,512]{1,0:T(8,128)(2,1)} %rows_ref.3) | copy-start | bytes 393220
  4.1 7.9 %collective-permute-start.1 = (bf16[8,128,512]{2,1,0:T(8,128)(2,1)S(1)}, bf16[8,128,512]{2,1,0:T(8,128)(2,1)S(1)}, u32[]{:S(2)}, u32[]{:S(2)}) collective-permute-start(bf16[8,128,512]{2,1,0:T(8,128)(2,1)S(1)} %shard_map.64), channel_id=1, source_target_pairs={{0,1},{1,0},{2,3},{3,2},{4,5},{5,4},{6,7},{7,6},{8,9},{9,8},{10,11... | collective-permute-start | bytes 3145736 | tf_op jit(solution)/shard_map/ppermute | solution.py:17
  7.1 10.9 %all-to-all-start = ((bf16[4,16,768]{2,1,0:T(8,128)(2,1)}), bf16[4,16,768]{2,1,0:T(8,128)(2,1)S(1)}, u32[]{:S(2)}, u32[]{:S(2)}) async-start(bf16[4,16,768]{2,1,0:T(8,128)(2,1)} %reshape.167), calls=%async_computation | async-start | bytes 196608 | tf_op jit(solution)/shard_map/all_to_all | solution.py:112
  12.0 1.0 copy-start.2
  13.0 19.3 %copy-start.5 = (s32[6144,1]{0,1:T(1,128)S(1)}, s32[6144,1]{0,1:T(1,128)}, u32[]{:S(2)}) copy-start(s32[6144,1]{0,1:T(1,128)} %param.11) | copy-start | bytes 73732
  17.3 50.8 %copy-start.3 = (bf16[128,512]{1,0:T(8,128)(2,1)S(1)}, bf16[128,512]{1,0:T(8,128)(2,1)}, u32[]{:S(2)}) copy-start(bf16[128,512]{1,0:T(8,128)(2,1)} %param.6) | copy-start | bytes 393220
  18.0 28.9 %all-to-all-start.1 = ((bf16[4,256,512]{2,1,0:T(8,128)(2,1)}), bf16[4,256,512]{2,1,0:T(8,128)(2,1)S(1)}, u32[]{:S(2)}, u32[]{:S(2)}) async-start(bf16[4,256,512]{2,1,0:T(8,128)(2,1)} %bitcast.3), calls=%async_computation.1 | async-start | bytes 2097152 | tf_op jit(solution)/shard_map/all_to_all | solution.py:140
  30.3 16.5 %collective-permute-start = (bf16[8,16,768]{2,1,0:T(8,128)(2,1)S(1)}, bf16[8,16,768]{2,1,0:T(8,128)(2,1)S(1)}, u32[]{:S(2)}, u32[]{:S(2)}) collective-permute-start(bf16[8,16,768]{2,1,0:T(8,128)(2,1)S(1)} %constant_dynamic-update-slice_fusion), channel_id=1, source_target_pairs={{0,2},{2,0},{1,3},{3,1},{4,6},{6,4},{5,7},{7,5},{8,10},{10,8},{9,1... | collective-permute-start | bytes 589832 | tf_op jit(solution)/shard_map/ppermute | solution.py:17
  47.1 22.0 %collective-permute-start.2 = (bf16[8,32,768]{2,1,0:T(8,128)(2,1)S(1)}, bf16[8,32,768]{2,1,0:T(8,128)(2,1)S(1)}, u32[]{:S(2)}, u32[]{:S(2)}) collective-permute-start(bf16[8,32,768]{2,1,0:T(8,128)(2,1)S(1)} %pad_maximum_fusion.1), channel_id=1, source_target_pairs={{0,4},{4,8},{8,12},{12,0},{1,5},{5,9},{9,13},{13,1},{2,6},{6,10},{... | collective-permute-start | bytes 1179656 | tf_op jit(solution)/shard_map/ppermute | solution.py:26
  49.3 19.8 %collective-permute-start.3 = (bf16[8,32,768]{2,1,0:T(8,128)(2,1)S(1)}, bf16[8,32,768]{2,1,0:T(8,128)(2,1)S(1)}, u32[]{:S(2)}, u32[]{:S(2)}) collective-permute-start(bf16[8,32,768]{2,1,0:T(8,128)(2,1)S(1)} %pad_maximum_fusion.1), channel_id=1, source_target_pairs={{0,8},{4,12},{8,0},{12,4},{1,9},{5,13},{9,1},{13,5},{2,10},{6,14},... | collective-permute-start | bytes 1179656 | tf_op jit(solution)/shard_map/ppermute | solution.py:26
  53.9 15.3 %collective-permute-start.4 = (bf16[8,32,768]{2,1,0:T(8,128)(2,1)S(1)}, bf16[8,32,768]{2,1,0:T(8,128)(2,1)S(1)}, u32[]{:S(2)}, u32[]{:S(2)}) collective-permute-start(bf16[8,32,768]{2,1,0:T(8,128)(2,1)S(1)} %pad_maximum_fusion.1), channel_id=1, source_target_pairs={{0,12},{4,0},{8,4},{12,8},{1,13},{5,1},{9,5},{13,9},{2,14},{6,2},{... | collective-permute-start | bytes 1179656 | tf_op jit(solution)/shard_map/ppermute | solution.py:26
  55.8 12.3 %collective-permute-start.5 = (bf16[128,512]{1,0:T(8,128)(2,1)S(1)}, bf16[128,512]{1,0:T(8,128)(2,1)S(1)}, u32[]{:S(2)}, u32[]{:S(2)}) collective-permute-start(bf16[128,512]{1,0:T(8,128)(2,1)S(1)} %fusion.16), channel_id=1, source_target_pairs={{0,2},{2,0},{1,3},{3,1},{4,6},{6,4},{5,7},{7,5},{8,10},{10,8},{9,1... | collective-permute-start | bytes 393224 | tf_op jit(solution)/shard_map/ppermute | solution.py:17
  69.2 17.9 %collective-permute-start.6 = (bf16[8,128,768]{2,1,0:T(8,128)(2,1)S(1)}, bf16[8,128,768]{2,1,0:T(8,128)(2,1)S(1)}, u32[]{:S(2)}, u32[]{:S(2)}) collective-permute-start(bf16[8,128,768]{2,1,0:T(8,128)(2,1)S(1)} %pad_maximum_fusion), channel_id=1, source_target_pairs={{0,1},{1,0},{2,3},{3,2},{4,5},{5,4},{6,7},{7,6},{8,9},{9,8},{10,11... | collective-permute-start | bytes 4718600 | tf_op jit(solution)/shard_map/ppermute | solution.py:17
  71.8 34.9 %all-to-all-start.2 = ((bf16[48,8,512]{2,1,0:T(8,128)(2,1)}), bf16[48,8,512]{2,1,0:T(8,128)(2,1)S(1)}, u32[]{:S(2)}, u32[]{:S(2)}) async-start(bf16[48,8,512]{2,1,0:T(8,128)(2,1)} %bitcast.27), calls=%async_computation.2 | async-start | bytes 786432 | tf_op jit(solution)/shard_map/all_to_all | solution.py:159
